TPU v7x, 32 devices: a whole 2x2x4 slice. The times are simulated.
32 devices in a mesh: grp: 4 (over y, x), blk: 8 (over z, core).
Axes of the slice: x: 2, y: 2, z: 4, core: 2. Of those that a mesh axis runs over, the one named last changes fastest.
Arguments:
- heads: bfloat16 [4096, 512], P(('grp', 'blk')), may hold values from -1.5 to 1.5
- tails: bfloat16 [65536, 512], P(('grp', 'blk')), may hold values from -1.5 to 1.5
- relation: bfloat16 [2304, 512], replicated, may hold values from -5 to 5
- head_block: int32 [8192], P(('grp', 'blk')), may hold values from 0 to 7
- tail_block: int32 [8192], P(('grp', 'blk')), may hold values from 0 to 15
- relation_id: int32 [8192], P(('grp', 'blk')), may hold values from 0 to 2303
- counts: int32 [8192, 128, 128], P(('grp', 'blk')), may hold values from 0 to 3
- owner: int32 [512, 1], P(('grp', 'blk')), may hold values from 0 to 3; in each aligned block of 16 rows (0 to 15, 16 to 31, ...) at most 8 rows name the same one
Outputs:
- head_grad: float32 [4096, 512], P(('grp', 'blk'))
- tail_grad: float32 [65536, 512], P(('grp', 'blk'))
Inputs may be any that keep to these rules, and one draw needn't show every extreme that they name: `owner`: among the 16 rows of one device no group is named more than 8 times.
All inputs are finite; a program needn't handle non-finite values.
Results may differ from a plain program's by a relative error of at most 0.0095.
Values may be sent and summed in bfloat16 or wider, within the bound.
A program may use at most 128 MiB of HBM per device.

v0:
```python
import jax
import jax.numpy as jnp
from jax import lax
from jax.sharding import PartitionSpec as P

grad_scale = 0.125


def local_pass(gathered, tails_local, relation, head_block, tail_block, relation_id, counts):
    tiles = head_block.shape[0]
    batch = min(16, tiles)
    turns = tiles // batch
    half = gathered.shape[2] // 2
    members = gathered.shape[0]
    blocks = tails_local.shape[0]
    kinds = relation.shape[0]
    items = (
        head_block.reshape(turns, batch),
        tail_block.reshape(turns, batch),
        relation_id.reshape(turns, batch),
        counts.reshape(turns, batch, counts.shape[1], counts.shape[2]),
    )

    def advance(carry, item):
        tail_acc, head_acc = carry
        hbk, tbk, rid, cnt = item
        head_pick = (hbk[:, None] == jnp.arange(members, dtype=jnp.int32)[None, :]).astype(
            jnp.bfloat16
        )
        tail_pick = (tbk[:, None] == jnp.arange(blocks, dtype=jnp.int32)[None, :]).astype(
            jnp.bfloat16
        )
        rel_pick = (rid[:, None] == jnp.arange(kinds, dtype=jnp.int32)[None, :]).astype(
            jnp.bfloat16
        )
        hblock = jnp.einsum("km,mid->kid", head_pick, gathered, preferred_element_type=jnp.float32)
        tblock = jnp.einsum(
            "kt,tid->kid", tail_pick, tails_local, preferred_element_type=jnp.float32
        ).astype(jnp.bfloat16)
        rel = jnp.dot(rel_pick, relation, preferred_element_type=jnp.float32)[:, None, :]
        h_re, h_im = (hblock[..., :half], hblock[..., half:])
        r_re, r_im = (rel[..., :half], rel[..., half:])
        query = jnp.concatenate(
            [h_re * r_re - h_im * r_im, h_re * r_im + h_im * r_re], axis=-1
        ).astype(jnp.bfloat16)
        scores = jnp.einsum("kid,kjd->kij", query, tblock, preferred_element_type=jnp.float32)
        weight = cnt.astype(jnp.float32)
        slope = (grad_scale * (jax.nn.sigmoid(scores) - weight * jax.nn.sigmoid(-scores))).astype(
            jnp.bfloat16
        )
        dtail = jnp.einsum("kij,kid->kjd", slope, query, preferred_element_type=jnp.float32)
        dquery = jnp.einsum("kij,kjd->kid", slope, tblock, preferred_element_type=jnp.float32)
        q_re, q_im = (dquery[..., :half], dquery[..., half:])
        dhead = jnp.concatenate([q_re * r_re + q_im * r_im, q_im * r_re - q_re * r_im], axis=-1)
        tail_acc = tail_acc + jnp.einsum(
            "kt,kjd->tjd", tail_pick.astype(jnp.float32), dtail, precision=lax.Precision.HIGHEST
        )
        head_acc = head_acc + jnp.einsum(
            "km,kid->mid", head_pick.astype(jnp.float32), dhead, precision=lax.Precision.HIGHEST
        )
        return ((tail_acc, head_acc), None)

    start = (jnp.zeros(tails_local.shape, jnp.float32), jnp.zeros(gathered.shape, jnp.float32))
    (tail_acc, head_acc), _ = lax.scan(advance, start, items)
    return (tail_acc, head_acc)


def on_device(heads, tails, relation, head_block, tail_block, relation_id, counts, owner):
    width = heads.shape[1]
    rows = heads.shape[0]
    members = lax.axis_size("blk")
    groups = lax.axis_size("grp")
    blocks = tails.shape[0] // rows
    gathered = lax.all_gather(heads, "blk", axis=0, tiled=True).reshape(members, rows, width)
    tails_local = tails.reshape(blocks, rows, width)
    tail_acc, head_acc = local_pass(
        gathered, tails_local, relation, head_block, tail_block, relation_id, counts
    )
    head_rows = head_acc.reshape(members * rows, width)
    head_grad = lax.psum_scatter(
        head_rows.astype(jnp.bfloat16), "blk", scatter_dimension=0, tiled=True
    ).astype(jnp.float32)
    tail_bf = tail_acc.astype(jnp.bfloat16)
    dest = owner[:, 0]
    onehot = (dest[:, None] == jnp.arange(groups, dtype=jnp.int32)[None, :]).astype(jnp.int32)
    dense = jnp.einsum(
        "tg,tid->gtid", onehot.astype(jnp.bfloat16), tail_bf, preferred_element_type=jnp.float32
    )
    summed = lax.psum_scatter(
        dense.reshape(groups * blocks, rows, width).astype(jnp.bfloat16),
        "grp",
        scatter_dimension=0,
        tiled=True,
    ).astype(jnp.float32)
    return (head_grad, summed.reshape(blocks * rows, width))


def solution(mesh):
    placed = (
        P(("grp", "blk"), None),
        P(("grp", "blk"), None),
        P(),
        P(("grp", "blk")),
        P(("grp", "blk")),
        P(("grp", "blk")),
        P(("grp", "blk"), None, None),
        P(("grp", "blk"), None),
    )
    return jax.shard_map(
        on_device,
        mesh=mesh,
        in_specs=placed,
        out_specs=(P(("grp", "blk"), None), P(("grp", "blk"), None)),
        check_vma=False,
    )
```

profile of v0, /device:TPU:0, one launch (start us, length us, event | category | flops | bytes accessed | tf_op | source)
XLA Modules:
  0.0 701.9 jit_solution(17685259364700438976)
XLA Ops:
  12.5 21.9 %all-gather.2.cloned.1.call-done = bf16[1024,512]{1,0:T(8,128)(2,1)} async-done(((bf16[128,512]{1,0:T(8,128)(2,1)}), bf16[1024,512]{1,0:T(8,128)(2,1)}) %all-gather.2.cloned.1.call-update) | async-done | bytes 1048592 | tf_op jit(solution)/shard_map/all_gather | solution.py:74
  36.2 531.9 %while.13 = (s32[]{:T(128)}, f32[16,128,512]{2,0,1:T(8,128)}, f32[8,128,512]{2,0,1:T(8,128)}, s32[16,16]{1,0:T(8,128)S(1)}, s32[16,16]{1,0:T(8,128)S(1)}, /*inde...) while((s32[]{:T(128)}, f32[16,128,512]{2,0,1:T(8,128)}, ...), condition=%wide.region_1.2_spmd.clone, body=%wide.region_0.1_spmd.clone.sunk | while | flops 1214812928 | bytes 105808840 | solution.py:64
  60.1 6.7 select_add_fusion.4
  91.1 9.0 %select_add_fusion.4 = f32[16,128,512]{2,0,1:T(8,128)} fusion(f32[16,128,512]{2,0,1:T(8,128)} %get-tuple-element.224, f32[16,128,512]{2,1,0:T(8,128)S(1)} %fusion.88, pred[]{:T(512)S(6)} %compare.3, s32[16]{0:T(128)S(1)} %get-tuple-element.201), kind=kOutput, calls=%fused_computation.6.clone.1 | convolution fusion | flops 203424000 | bytes 12582977 | tf_op jit(solution)/shard_map/while/body/eval_jaxpr/kt,kjd->tjd/dot_general | solution.py:55
  124.6 9.0 %select_add_fusion.4 = f32[16,128,512]{2,0,1:T(8,128)} fusion(f32[16,128,512]{2,0,1:T(8,128)} %get-tuple-element.224, f32[16,128,512]{2,1,0:T(8,128)S(1)} %fusion.88, pred[]{:T(512)S(6)} %compare.3, s32[16]{0:T(128)S(1)} %get-tuple-element.201), kind=kOutput, calls=%fused_computation.6.clone.1 | convolution fusion | flops 203424000 | bytes 12582977 | tf_op jit(solution)/shard_map/while/body/eval_jaxpr/kt,kjd->tjd/dot_general | solution.py:55
  158.0 9.0 %select_add_fusion.4 = f32[16,128,512]{2,0,1:T(8,128)} fusion(f32[16,128,512]{2,0,1:T(8,128)} %get-tuple-element.224, f32[16,128,512]{2,1,0:T(8,128)S(1)} %fusion.88, pred[]{:T(512)S(6)} %compare.3, s32[16]{0:T(128)S(1)} %get-tuple-element.201), kind=kOutput, calls=%fused_computation.6.clone.1 | convolution fusion | flops 203424000 | bytes 12582977 | tf_op jit(solution)/shard_map/while/body/eval_jaxpr/kt,kjd->tjd/dot_general | solution.py:55
  191.4 9.0 %select_add_fusion.4 = f32[16,128,512]{2,0,1:T(8,128)} fusion(f32[16,128,512]{2,0,1:T(8,128)} %get-tuple-element.224, f32[16,128,512]{2,1,0:T(8,128)S(1)} %fusion.88, pred[]{:T(512)S(6)} %compare.3, s32[16]{0:T(128)S(1)} %get-tuple-element.201), kind=kOutput, calls=%fused_computation.6.clone.1 | convolution fusion | flops 203424000 | bytes 12582977 | tf_op jit(solution)/shard_map/while/body/eval_jaxpr/kt,kjd->tjd/dot_general | solution.py:55
  216.3 5.9 select_add_fusion.5
  224.9 9.0 %select_add_fusion.4 = f32[16,128,512]{2,0,1:T(8,128)} fusion(f32[16,128,512]{2,0,1:T(8,128)} %get-tuple-element.224, f32[16,128,512]{2,1,0:T(8,128)S(1)} %fusion.88, pred[]{:T(512)S(6)} %compare.3, s32[16]{0:T(128)S(1)} %get-tuple-element.201), kind=kOutput, calls=%fused_computation.6.clone.1 | convolution fusion | flops 203424000 | bytes 12582977 | tf_op jit(solution)/shard_map/while/body/eval_jaxpr/kt,kjd->tjd/dot_general | solution.py:55
  249.8 5.9 select_add_fusion.5
  258.3 9.0 %select_add_fusion.4 = f32[16,128,512]{2,0,1:T(8,128)} fusion(f32[16,128,512]{2,0,1:T(8,128)} %get-tuple-element.224, f32[16,128,512]{2,1,0:T(8,128)S(1)} %fusion.88, pred[]{:T(512)S(6)} %compare.3, s32[16]{0:T(128)S(1)} %get-tuple-element.201), kind=kOutput, calls=%fused_computation.6.clone.1 | convolution fusion | flops 203424000 | bytes 12582977 | tf_op jit(solution)/shard_map/while/body/eval_jaxpr/kt,kjd->tjd/dot_general | solution.py:55
  283.2 5.9 select_add_fusion.5
  291.7 9.0 %select_add_fusion.4 = f32[16,128,512]{2,0,1:T(8,128)} fusion(f32[16,128,512]{2,0,1:T(8,128)} %get-tuple-element.224, f32[16,128,512]{2,1,0:T(8,128)S(1)} %fusion.88, pred[]{:T(512)S(6)} %compare.3, s32[16]{0:T(128)S(1)} %get-tuple-element.201), kind=kOutput, calls=%fused_computation.6.clone.1 | convolution fusion | flops 203424000 | bytes 12582977 | tf_op jit(solution)/shard_map/while/body/eval_jaxpr/kt,kjd->tjd/dot_general | solution.py:55
  325.2 9.0 %select_add_fusion.4 = f32[16,128,512]{2,0,1:T(8,128)} fusion(f32[16,128,512]{2,0,1:T(8,128)} %get-tuple-element.224, f32[16,128,512]{2,1,0:T(8,128)S(1)} %fusion.88, pred[]{:T(512)S(6)} %compare.3, s32[16]{0:T(128)S(1)} %get-tuple-element.201), kind=kOutput, calls=%fused_computation.6.clone.1 | convolution fusion | flops 203424000 | bytes 12582977 | tf_op jit(solution)/shard_map/while/body/eval_jaxpr/kt,kjd->tjd/dot_general | solution.py:55
  358.6 9.0 %select_add_fusion.4 = f32[16,128,512]{2,0,1:T(8,128)} fusion(f32[16,128,512]{2,0,1:T(8,128)} %get-tuple-element.224, f32[16,128,512]{2,1,0:T(8,128)S(1)} %fusion.88, pred[]{:T(512)S(6)} %compare.3, s32[16]{0:T(128)S(1)} %get-tuple-element.201), kind=kOutput, calls=%fused_computation.6.clone.1 | convolution fusion | flops 203424000 | bytes 12582977 | tf_op jit(solution)/shard_map/while/body/eval_jaxpr/kt,kjd->tjd/dot_general | solution.py:55
  392.0 9.0 %select_add_fusion.4 = f32[16,128,512]{2,0,1:T(8,128)} fusion(f32[16,128,512]{2,0,1:T(8,128)} %get-tuple-element.224, f32[16,128,512]{2,1,0:T(8,128)S(1)} %fusion.88, pred[]{:T(512)S(6)} %compare.3, s32[16]{0:T(128)S(1)} %get-tuple-element.201), kind=kOutput, calls=%fused_computation.6.clone.1 | convolution fusion | flops 203424000 | bytes 12582977 | tf_op jit(solution)/shard_map/while/body/eval_jaxpr/kt,kjd->tjd/dot_general | solution.py:55
  425.5 9.0 %select_add_fusion.4 = f32[16,128,512]{2,0,1:T(8,128)} fusion(f32[16,128,512]{2,0,1:T(8,128)} %get-tuple-element.224, f32[16,128,512]{2,1,0:T(8,128)S(1)} %fusion.88, pred[]{:T(512)S(6)} %compare.3, s32[16]{0:T(128)S(1)} %get-tuple-element.201), kind=kOutput, calls=%fused_computation.6.clone.1 | convolution fusion | flops 203424000 | bytes 12582977 | tf_op jit(solution)/shard_map/while/body/eval_jaxpr/kt,kjd->tjd/dot_general | solution.py:55
  458.9 9.0 %select_add_fusion.4 = f32[16,128,512]{2,0,1:T(8,128)} fusion(f32[16,128,512]{2,0,1:T(8,128)} %get-tuple-element.224, f32[16,128,512]{2,1,0:T(8,128)S(1)} %fusion.88, pred[]{:T(512)S(6)} %compare.3, s32[16]{0:T(128)S(1)} %get-tuple-element.201), kind=kOutput, calls=%fused_computation.6.clone.1 | convolution fusion | flops 203424000 | bytes 12582977 | tf_op jit(solution)/shard_map/while/body/eval_jaxpr/kt,kjd->tjd/dot_general | solution.py:55
  492.3 9.0 %select_add_fusion.4 = f32[16,128,512]{2,0,1:T(8,128)} fusion(f32[16,128,512]{2,0,1:T(8,128)} %get-tuple-element.224, f32[16,128,512]{2,1,0:T(8,128)S(1)} %fusion.88, pred[]{:T(512)S(6)} %compare.3, s32[16]{0:T(128)S(1)} %get-tuple-element.201), kind=kOutput, calls=%fused_computation.6.clone.1 | convolution fusion | flops 203424000 | bytes 12582977 | tf_op jit(solution)/shard_map/while/body/eval_jaxpr/kt,kjd->tjd/dot_general | solution.py:55
  525.8 9.0 %select_add_fusion.4 = f32[16,128,512]{2,0,1:T(8,128)} fusion(f32[16,128,512]{2,0,1:T(8,128)} %get-tuple-element.224, f32[16,128,512]{2,1,0:T(8,128)S(1)} %fusion.88, pred[]{:T(512)S(6)} %compare.3, s32[16]{0:T(128)S(1)} %get-tuple-element.201), kind=kOutput, calls=%fused_computation.6.clone.1 | convolution fusion | flops 203424000 | bytes 12582977 | tf_op jit(solution)/shard_map/while/body/eval_jaxpr/kt,kjd->tjd/dot_general | solution.py:55
  559.2 9.0 %select_add_fusion.4 = f32[16,128,512]{2,0,1:T(8,128)} fusion(f32[16,128,512]{2,0,1:T(8,128)} %get-tuple-element.224, f32[16,128,512]{2,1,0:T(8,128)S(1)} %fusion.88, pred[]{:T(512)S(6)} %compare.3, s32[16]{0:T(128)S(1)} %get-tuple-element.201), kind=kOutput, calls=%fused_computation.6.clone.1 | convolution fusion | flops 203424000 | bytes 12582977 | tf_op jit(solution)/shard_map/while/body/eval_jaxpr/kt,kjd->tjd/dot_general | solution.py:55
  576.4 6.2 multiply_convert_fusion
  582.6 20.9 %reduce-scatter.3.cloned.1.call-done = bf16[128,512]{1,0:T(8,128)(2,1)} async-done(((bf16[1024,512]{1,0:T(8,128)(2,1)}), bf16[128,512]{1,0:T(8,128)(2,1)}) %reduce-scatter.3.cloned.1.call-update) | async-done | bytes 131088 | tf_op jit(solution)/shard_map/reduce_scatter | solution.py:80
  605.1 86.1 %reduce-scatter.5.cloned.1.call-done = bf16[16,128,512]{2,1,0:T(8,128)(2,1)} async-done(((bf16[64,128,512]{2,1,0:T(8,128)(2,1)}), bf16[16,128,512]{2,1,0:T(8,128)(2,1)}) %reduce-scatter.5.cloned.1.call-update) | async-done | bytes 2097168 | tf_op jit(solution)/shard_map/reduce_scatter | solution.py:89
  (379 shorter events, 392.4 us)
Async XLA Ops:
  7.2 27.3 %all-gather.2.cloned.1.call-start = ((), (), s32[]{:S(2)}) async-start(), calls=%async_computation.2 | async-start | bytes 1179648 | tf_op jit(solution)/shard_map/all_gather | solution.py:74
  7.9 595.6 %reduce-scatter.3.cloned.1.call-start = ((), (), s32[]{:S(2)}) async-start(), calls=%async_computation.3 | async-start | bytes 1179648 | tf_op jit(solution)/shard_map/reduce_scatter | solution.py:80
  8.0 28.2 %copy-start.1 = (bf16[2304,512]{1,0:T(8,128)(2,1)S(1)}, bf16[2304,512]{1,0:T(8,128)(2,1)}, u32[]{:S(2)}) copy-start(bf16[2304,512]{1,0:T(8,128)(2,1)} %param.12) | copy-start | bytes 7077892
  91.1 9.0 %copy-start.2 = (bf16[2304,512]{1,0:T(8,128)(2,1)S(1)}, bf16[2304,512]{1,0:T(8,128)(2,1)}, u32[]{:S(2)}) copy-start(bf16[2304,512]{1,0:T(8,128)(2,1)} %get-tuple-element.262) | copy-start | bytes 7077892 | tf_op jit(solution)/shard_map/while
  91.1 9.0 %copy-start.4 = (bf16[8,128,512]{2,0,1:T(8,128)(2,1)S(1)}, bf16[8,128,512]{2,0,1:T(8,128)(2,1)}, u32[]{:S(2)}) copy-start(bf16[8,128,512]{2,0,1:T(8,128)(2,1)} %copy-done.3) | copy-start | bytes 3145732 | tf_op jit(solution)/shard_map/while
  124.6 9.0 %copy-start.2 = (bf16[2304,512]{1,0:T(8,128)(2,1)S(1)}, bf16[2304,512]{1,0:T(8,128)(2,1)}, u32[]{:S(2)}) copy-start(bf16[2304,512]{1,0:T(8,128)(2,1)} %get-tuple-element.262) | copy-start | bytes 7077892 | tf_op jit(solution)/shard_map/while
  158.0 9.0 %copy-start.2 = (bf16[2304,512]{1,0:T(8,128)(2,1)S(1)}, bf16[2304,512]{1,0:T(8,128)(2,1)}, u32[]{:S(2)}) copy-start(bf16[2304,512]{1,0:T(8,128)(2,1)} %get-tuple-element.262) | copy-start | bytes 7077892 | tf_op jit(solution)/shard_map/while
  191.4 9.0 %copy-start.2 = (bf16[2304,512]{1,0:T(8,128)(2,1)S(1)}, bf16[2304,512]{1,0:T(8,128)(2,1)}, u32[]{:S(2)}) copy-start(bf16[2304,512]{1,0:T(8,128)(2,1)} %get-tuple-element.262) | copy-start | bytes 7077892 | tf_op jit(solution)/shard_map/while
  224.9 9.0 %copy-start.2 = (bf16[2304,512]{1,0:T(8,128)(2,1)S(1)}, bf16[2304,512]{1,0:T(8,128)(2,1)}, u32[]{:S(2)}) copy-start(bf16[2304,512]{1,0:T(8,128)(2,1)} %get-tuple-element.262) | copy-start | bytes 7077892 | tf_op jit(solution)/shard_map/while
  258.3 9.0 %copy-start.2 = (bf16[2304,512]{1,0:T(8,128)(2,1)S(1)}, bf16[2304,512]{1,0:T(8,128)(2,1)}, u32[]{:S(2)}) copy-start(bf16[2304,512]{1,0:T(8,128)(2,1)} %get-tuple-element.262) | copy-start | bytes 7077892 | tf_op jit(solution)/shard_map/while
  291.7 9.0 %copy-start.2 = (bf16[2304,512]{1,0:T(8,128)(2,1)S(1)}, bf16[2304,512]{1,0:T(8,128)(2,1)}, u32[]{:S(2)}) copy-start(bf16[2304,512]{1,0:T(8,128)(2,1)} %get-tuple-element.262) | copy-start | bytes 7077892 | tf_op jit(solution)/shard_map/while
  325.1 9.0 %copy-start.2 = (bf16[2304,512]{1,0:T(8,128)(2,1)S(1)}, bf16[2304,512]{1,0:T(8,128)(2,1)}, u32[]{:S(2)}) copy-start(bf16[2304,512]{1,0:T(8,128)(2,1)} %get-tuple-element.262) | copy-start | bytes 7077892 | tf_op jit(solution)/shard_map/while
  358.6 9.0 %copy-start.2 = (bf16[2304,512]{1,0:T(8,128)(2,1)S(1)}, bf16[2304,512]{1,0:T(8,128)(2,1)}, u32[]{:S(2)}) copy-start(bf16[2304,512]{1,0:T(8,128)(2,1)} %get-tuple-element.262) | copy-start | bytes 7077892 | tf_op jit(solution)/shard_map/while
  358.6 9.0 %copy-start.4 = (bf16[8,128,512]{2,0,1:T(8,128)(2,1)S(1)}, bf16[8,128,512]{2,0,1:T(8,128)(2,1)}, u32[]{:S(2)}) copy-start(bf16[8,128,512]{2,0,1:T(8,128)(2,1)} %copy-done.3) | copy-start | bytes 3145732 | tf_op jit(solution)/shard_map/while
  392.0 9.0 %copy-start.2 = (bf16[2304,512]{1,0:T(8,128)(2,1)S(1)}, bf16[2304,512]{1,0:T(8,128)(2,1)}, u32[]{:S(2)}) copy-start(bf16[2304,512]{1,0:T(8,128)(2,1)} %get-tuple-element.262) | copy-start | bytes 7077892 | tf_op jit(solution)/shard_map/while
  392.0 9.0 %copy-start.4 = (bf16[8,128,512]{2,0,1:T(8,128)(2,1)S(1)}, bf16[8,128,512]{2,0,1:T(8,128)(2,1)}, u32[]{:S(2)}) copy-start(bf16[8,128,512]{2,0,1:T(8,128)(2,1)} %copy-done.3) | copy-start | bytes 3145732 | tf_op jit(solution)/shard_map/while
  425.4 9.0 %copy-start.2 = (bf16[2304,512]{1,0:T(8,128)(2,1)S(1)}, bf16[2304,512]{1,0:T(8,128)(2,1)}, u32[]{:S(2)}) copy-start(bf16[2304,512]{1,0:T(8,128)(2,1)} %get-tuple-element.262) | copy-start | bytes 7077892 | tf_op jit(solution)/shard_map/while
  425.5 9.0 %copy-start.4 = (bf16[8,128,512]{2,0,1:T(8,128)(2,1)S(1)}, bf16[8,128,512]{2,0,1:T(8,128)(2,1)}, u32[]{:S(2)}) copy-start(bf16[8,128,512]{2,0,1:T(8,128)(2,1)} %copy-done.3) | copy-start | bytes 3145732 | tf_op jit(solution)/shard_map/while
  458.9 9.0 %copy-start.2 = (bf16[2304,512]{1,0:T(8,128)(2,1)S(1)}, bf16[2304,512]{1,0:T(8,128)(2,1)}, u32[]{:S(2)}) copy-start(bf16[2304,512]{1,0:T(8,128)(2,1)} %get-tuple-element.262) | copy-start | bytes 7077892 | tf_op jit(solution)/shard_map/while
  458.9 9.0 %copy-start.4 = (bf16[8,128,512]{2,0,1:T(8,128)(2,1)S(1)}, bf16[8,128,512]{2,0,1:T(8,128)(2,1)}, u32[]{:S(2)}) copy-start(bf16[8,128,512]{2,0,1:T(8,128)(2,1)} %copy-done.3) | copy-start | bytes 3145732 | tf_op jit(solution)/shard_map/while
  492.3 9.0 %copy-start.2 = (bf16[2304,512]{1,0:T(8,128)(2,1)S(1)}, bf16[2304,512]{1,0:T(8,128)(2,1)}, u32[]{:S(2)}) copy-start(bf16[2304,512]{1,0:T(8,128)(2,1)} %get-tuple-element.262) | copy-start | bytes 7077892 | tf_op jit(solution)/shard_map/while
  525.7 9.0 %copy-start.2 = (bf16[2304,512]{1,0:T(8,128)(2,1)S(1)}, bf16[2304,512]{1,0:T(8,128)(2,1)}, u32[]{:S(2)}) copy-start(bf16[2304,512]{1,0:T(8,128)(2,1)} %get-tuple-element.262) | copy-start | bytes 7077892 | tf_op jit(solution)/shard_map/while
  559.2 9.0 %copy-start.2 = (bf16[2304,512]{1,0:T(8,128)(2,1)S(1)}, bf16[2304,512]{1,0:T(8,128)(2,1)}, u32[]{:S(2)}) copy-start(bf16[2304,512]{1,0:T(8,128)(2,1)} %get-tuple-element.262) | copy-start | bytes 7077892 | tf_op jit(solution)/shard_map/while
  571.3 119.9 %reduce-scatter.5.cloned.1.call-start = ((), (), s32[]{:S(2)}) async-start(), calls=%async_computation.4 | async-start | bytes 10485760 | tf_op jit(solution)/shard_map/reduce_scatter | solution.py:89
  (48 other events, 160.2 us)
Sparse Core Ops, SparseCore 0:
  9.6 24.7 all-gather.1
  571.4 32.0 reduce-scatter.2
  606.5 84.6 reduce-scatter.4
where the time goes:
time: 703 us; the launch traced here: 702 us
  matrix products  412 us (59%)
  waiting for transfers between devices  130 us (18%)
  other arithmetic  101 us (14%)
  local copies, waits for them, and re-layouts  44.8 us (6%)
  between operations  13.8 us (2%)
    dot_general x16, matrix products, advance(): jnp.einsum('kt,kjd->tjd', tail_pick.astype(jnp.float32), dtail, precision...  142 us
    dot_general x16, matrix products, advance(): jnp.einsum('km,kid->mid', head_pick.astype(jnp.float32), dhead, precision...  93.3 us
    reduce_scatter x1, waiting for transfers between devices, on_device(): lax.psum_scatter(dense.reshape(groups * blocks, rows, width).astype(jnp.b...  86.1 us
    add x16, other arithmetic, advance(): q_re * r_re + q_im * r_im  69.7 us
    dot_general x16, matrix products, advance(): jnp.einsum('kid,kjd->kij', query, tblock, preferred_element_type=jnp.floa...  60.8 us
    dot_general x16, matrix products, advance(): jnp.einsum('kij,kid->kjd', slope, query, preferred_element_type=jnp.float32)  42.4 us
    dot_general x16, matrix products, advance(): jnp.einsum('kij,kjd->kid', slope, tblock, preferred_element_type=jnp.floa...  42.2 us
    while x128, local copies, waits for them, and re-layouts  25.3 us
  transfers between devices with their start and end apart: 3, of which 3 were waited for; matrix products, arithmetic and copies ran while one was open for 2% of the time, Pallas kernels for 0%

commit v1 on v0

v1 whole, which is shorter than its diff:
```python
import functools

import jax
import jax.numpy as jnp
from jax import lax
from jax.experimental import pallas as pl
from jax.experimental.pallas import tpu as pltpu
from jax.sharding import PartitionSpec as P

grad_scale = 0.125
GROUP = 4
DEPTH = 4
CHUNKS = 4


def group_lists(names, kinds, size):
    tiles = names.shape[0]
    k = jnp.arange(tiles, dtype=jnp.int32)
    same = names[:, None] == names[None, :]
    place = jnp.sum((same & (k[None, :] < k[:, None])).astype(jnp.int32), axis=1)
    t = jnp.arange(kinds + 1, dtype=jnp.int32)
    number = jnp.sum((names[None, :] == t[:, None]).astype(jnp.int32), axis=1)
    groups = (number + size - 1) // size
    start = jnp.sum(jnp.where(t[None, :] < t[:, None], groups[None, :], 0), axis=1)
    base = jnp.sum(jnp.where(names[:, None] == t[None, :], start[None, :], 0), axis=1)
    spot = base * size + place
    total = (tiles // size + kinds) * size
    p = jnp.arange(total, dtype=jnp.int32)
    listing = jnp.sum(jnp.where(spot[None, :] == p[:, None], k[None, :] + 1, 0), axis=1) - 1
    return listing, start


def tail_kernel(first, list_ref, gs_ref, hb_ref, heads_ref, tails_ref, rel_ref, counts_ref, *rest):
    tail_out, slope_out, cbuf, sbuf, acc, csem, ssem = rest[-7:]
    own = tails_ref.shape[0]
    half = tails_ref.shape[2] // 2
    begin = gs_ref[first]
    end = gs_ref[first + own]

    def fetch(j, slot):
        for g in range(GROUP):
            k = jnp.maximum(list_ref[j * GROUP + g], 0)
            pltpu.make_async_copy(counts_ref.at[k], cbuf.at[slot, g], csem.at[slot, g]).start()

    def settle(slot):
        for g in range(GROUP):
            pltpu.make_async_copy(sbuf.at[slot, g], slope_out.at[0], ssem.at[slot, g]).wait()

    for d in range(DEPTH - 1):
        @pl.when(begin + d < end)
        def _():
            fetch(begin + d, d)

    def body(t, j):
        step = j - begin
        slot = lax.rem(step, DEPTH)
        out = lax.rem(step, 2)
        ahead = j + DEPTH - 1

        @pl.when(ahead < end)
        def _():
            fetch(ahead, lax.rem(step + DEPTH - 1, DEPTH))

        @pl.when(step >= 2)
        def _():
            settle(out)

        for g in range(GROUP):
            pltpu.make_async_copy(counts_ref.at[0], cbuf.at[slot, g], csem.at[slot, g]).wait()
        tail = tails_ref[t]
        queries, slopes = [], []
        for g in range(GROUP):
            entry = list_ref[j * GROUP + g]
            k = jnp.maximum(entry, 0)
            scale = jnp.where(entry >= 0, 0.5 * grad_scale, 0.0).astype(jnp.float32)
            h = heads_ref[hb_ref[k]]
            r = rel_ref[pl.ds(k, 1), :].astype(jnp.bfloat16)
            h_re, h_im = h[:, :half], h[:, half:]
            r_re, r_im = r[:, :half], r[:, half:]
            q = jnp.concatenate([h_re * r_re - h_im * r_im, h_re * r_im + h_im * r_re], axis=1)
            s = lax.dot_general(q, tail, (((1,), (1,)), ((), ())), preferred_element_type=jnp.float32)
            w = cbuf[slot, g].astype(jnp.float32) * scale
            slope = ((scale - w) + jnp.tanh(0.5 * s) * (scale + w)).astype(jnp.bfloat16)
            sbuf[out, g] = slope
            queries.append(q)
            slopes.append(slope)
        acc[...] += lax.dot_general(
            jnp.concatenate(slopes, axis=0),
            jnp.concatenate(queries, axis=0),
            (((0,), (0,)), ((), ())),
            preferred_element_type=jnp.float32,
        )
        for g in range(GROUP):
            entry = list_ref[j * GROUP + g]
            k = jnp.where(entry >= 0, entry, slope_out.shape[0] - 1)
            pltpu.make_async_copy(sbuf.at[out, g], slope_out.at[k], ssem.at[out, g]).start()

    def per_tail(t, carry):
        acc[...] = jnp.zeros_like(acc)

        def inner(j, c):
            body(t, j)
            return c

        lax.fori_loop(gs_ref[first + t], gs_ref[first + t + 1], inner, 0)
        tail_out[t] = acc[...].astype(jnp.bfloat16)
        return carry

    lax.fori_loop(0, own, per_tail, 0)
    steps = end - begin
    for back in (2, 1):
        @pl.when(steps >= back)
        def _():
            settle(lax.rem(steps - back, 2))


def head_kernel(list_ref, gs_ref, tb_ref, tails_ref, rel_ref, slope_ref, head_out, buf, acc, sem):
    members = head_out.shape[0]
    half = tails_ref.shape[2] // 2
    end = gs_ref[members]

    def fetch(j, slot):
        for g in range(GROUP):
            k = jnp.maximum(list_ref[j * GROUP + g], 0)
            pltpu.make_async_copy(slope_ref.at[k], buf.at[slot, g], sem.at[slot, g]).start()

    for d in range(DEPTH - 1):
        @pl.when(d < end)
        def _():
            fetch(d, d)

    def body(j):
        slot = lax.rem(j, DEPTH)

        @pl.when(j + DEPTH - 1 < end)
        def _():
            fetch(j + DEPTH - 1, lax.rem(j + DEPTH - 1, DEPTH))

        for g in range(GROUP):
            pltpu.make_async_copy(slope_ref.at[0], buf.at[slot, g], sem.at[slot, g]).wait()
        turned, slopes = [], []
        for g in range(GROUP):
            entry = list_ref[j * GROUP + g]
            k = jnp.maximum(entry, 0)
            t = tails_ref[tb_ref[k]]
            keep = jnp.where(entry >= 0, 1.0, 0.0).astype(jnp.float32)
            r = (rel_ref[pl.ds(k, 1), :] * keep).astype(jnp.bfloat16)
            t_re, t_im = t[:, :half], t[:, half:]
            r_re, r_im = r[:, :half], r[:, half:]
            turned.append(
                jnp.concatenate([t_re * r_re + t_im * r_im, t_im * r_re - t_re * r_im], axis=1)
            )
            slopes.append(buf[slot, g])
        acc[...] += jnp.dot(
            jnp.concatenate(slopes, axis=1),
            jnp.concatenate(turned, axis=0),
            preferred_element_type=jnp.float32,
        )

    def per_head(h, carry):
        acc[...] = jnp.zeros_like(acc)

        def inner(j, c):
            body(j)
            return c

        lax.fori_loop(gs_ref[h], gs_ref[h + 1], inner, 0)
        head_out[h] = acc[...].astype(jnp.bfloat16)
        return carry

    lax.fori_loop(0, members, per_head, 0)


smem = pl.BlockSpec(memory_space=pltpu.SMEM)
vmem = pl.BlockSpec(memory_space=pltpu.VMEM)
hbm = pl.BlockSpec(memory_space=pl.ANY)


def tail_chunk(first, own, listing, starts, hb, heads, tails, rel, counts, slopes):
    tiles, rows, _ = counts.shape
    width = tails.shape[2]
    work = tiles * own // 16
    args = [listing, starts, hb, heads, tails, rel, counts]
    specs = [smem, smem, smem, vmem, vmem, vmem, hbm]
    aliases = {}
    if slopes is not None:
        args.append(slopes)
        specs.append(hbm)
        aliases = {len(args) - 1: 1}
    return pl.pallas_call(
        functools.partial(tail_kernel, first),
        out_shape=[
            jax.ShapeDtypeStruct((own, rows, width), jnp.bfloat16),
            jax.ShapeDtypeStruct((tiles + 1, rows, rows), jnp.bfloat16),
        ],
        in_specs=specs,
        out_specs=[vmem, hbm],
        scratch_shapes=[
            pltpu.VMEM((DEPTH, GROUP, rows, rows), jnp.int32),
            pltpu.VMEM((2, GROUP, rows, rows), jnp.bfloat16),
            pltpu.VMEM((rows, width), jnp.float32),
            pltpu.SemaphoreType.DMA((DEPTH, GROUP)),
            pltpu.SemaphoreType.DMA((2, GROUP)),
        ],
        input_output_aliases=aliases,
        compiler_params=pltpu.CompilerParams(vmem_limit_bytes=32 * 1024 * 1024),
        cost_estimate=pl.CostEstimate(
            flops=8 * work * rows * rows * width,
            bytes_accessed=work * rows * rows * 6,
            transcendentals=work * rows * rows,
        ),
        name="tail_chunk",
    )(*args)


def head_pass(members, listing, starts, tb, tails, rel, slopes):
    _, rows, width = tails.shape
    work = slopes.shape[0]
    return pl.pallas_call(
        head_kernel,
        out_shape=jax.ShapeDtypeStruct((members, rows, width), jnp.bfloat16),
        in_specs=[smem, smem, smem, vmem, vmem, hbm],
        out_specs=vmem,
        scratch_shapes=[
            pltpu.VMEM((DEPTH, GROUP, rows, rows), jnp.bfloat16),
            pltpu.VMEM((rows, width), jnp.float32),
            pltpu.SemaphoreType.DMA((DEPTH, GROUP)),
        ],
        compiler_params=pltpu.CompilerParams(vmem_limit_bytes=32 * 1024 * 1024),
        cost_estimate=pl.CostEstimate(
            flops=4 * work * rows * rows * width,
            bytes_accessed=work * rows * rows * 2,
            transcendentals=0,
        ),
        name="head_pass",
    )(listing, starts, tb, tails, rel, slopes)


def on_device(heads, tails, relation, head_block, tail_block, relation_id, counts, owner):
    rows, width = heads.shape
    members = lax.axis_size("blk")
    groups = lax.axis_size("grp")
    blocks = tails.shape[0] // rows
    me = lax.axis_index("grp")
    gathered = lax.all_gather(heads, "blk", axis=0, tiled=True).reshape(members, rows, width)
    owners = lax.all_gather(owner[:, 0], "grp", axis=0)
    tails3 = tails.reshape(blocks, rows, width)
    kinds = jnp.arange(relation.shape[0], dtype=jnp.int32)
    pick = (relation_id[:, None] == kinds[None, :]).astype(jnp.bfloat16)
    rel = jnp.dot(pick, relation, preferred_element_type=jnp.float32)
    by_tail, tail_starts = group_lists(tail_block, blocks, GROUP)
    by_head, head_starts = group_lists(head_block, members, GROUP)

    own = blocks // CHUNKS
    slopes = None
    parts = []
    for c in range(CHUNKS):
        part, slopes = tail_chunk(
            c * own, own, by_tail, tail_starts, head_block, gathered,
            tails3[c * own : (c + 1) * own], rel, counts, slopes,
        )
        parts.append(part)

    head_local = head_pass(members, by_head, head_starts, tail_block, tails3, rel, slopes)
    head_grad = lax.psum_scatter(
        head_local.reshape(members * rows, width), "blk", scatter_dimension=0, tiled=True
    ).astype(jnp.float32)

    def named(source, target, at, count):
        route = lax.dynamic_slice_in_dim(
            lax.dynamic_index_in_dim(owners, source, 0, keepdims=False), at, count
        )
        return (route == target)[:, None, None]

    def take(mask, value):
        return jnp.where(mask, value.astype(jnp.float32), 0.0)

    piece = own // 2
    outs = []
    for c in range(CHUNKS):
        for side in range(2):
            near, far = (1, 2) if side == 0 else (2, 1)
            at = c * own + side * piece
            mine = parts[c][side * piece : (side + 1) * piece]
            theirs = lax.ppermute(mine, "grp", [(g, g ^ near) for g in range(groups)])
            onward = (
                take(named(me, me ^ far, at, piece), mine)
                + take(named(me ^ near, me ^ far, at, piece), theirs)
            ).astype(jnp.bfloat16)
            last = lax.ppermute(onward, "grp", [(g, g ^ far) for g in range(groups)])
            outs.append(
                take(named(me, me, at, piece), mine)
                + take(named(me ^ near, me, at, piece), theirs)
                + last.astype(jnp.float32)
            )
    tail_grad = jnp.concatenate(outs, axis=0).reshape(blocks * rows, width)
    return (head_grad, tail_grad)


def solution(mesh):
    placed = (
        P(("grp", "blk"), None),
        P(("grp", "blk"), None),
        P(),
        P(("grp", "blk")),
        P(("grp", "blk")),
        P(("grp", "blk")),
        P(("grp", "blk"), None, None),
        P(("grp", "blk"), None),
    )
    return jax.shard_map(
        on_device,
        mesh=mesh,
        in_specs=placed,
        out_specs=(P(("grp", "blk"), None), P(("grp", "blk"), None)),
        check_vma=False,
    )
```

time: 703 us -> 199 us (0.28)
  matrix products: 412 us -> 0.82 us
  waiting for transfers between devices: 130 us -> 31.8 us
  Pallas kernels: 0 us -> 92.7 us
  other arithmetic: 101 us -> 20.8 us
  local copies, waits for them, and re-layouts: 44.8 us -> 9.95 us
  starting transfers between devices: 0.12 us -> 18.1 us
  blocking collectives: 0 us -> 8.82 us
    dot_general x128 -> x1, matrix products: 412 us -> 0.82 us  [on_device(): rel = jnp.dot(pick, relation, preferred_element_type=jnp.float32)]
    reduce_scatter x2 -> x1, waiting for transfers between devices: 107 us -> 0.01 us  [on_device(): lax.psum_scatter(head_local.reshape(members * rows, width), 'blk', scatte...]
    pallas_call x0 -> x5, Pallas kernels: none -> 92.7 us  [the longest x4 59.9 us: tail_chunk(): pl.pallas_call(functools.partial(tail_kernel, first), out_shape=[jax.Shap...]
    add x16 -> x2, other arithmetic: 69.7 us -> 0.01 us  [group_lists(): spot = base * size + place]
    ppermute x0 -> x16, waiting for transfers between devices: none -> 26 us  [the longest x8 17.7 us: on_device(): last = lax.ppermute(onward, 'grp', [(g, g ^ far) for g in range(groups)])]
    while x128 -> x0, local copies, waits for them, and re-layouts: 25.3 us -> none
    ppermute x0 -> x16, starting transfers between devices: none -> 18 us  [the longest x8 9.42 us: on_device(): theirs = lax.ppermute(mine, 'grp', [(g, g ^ near) for g in range(groups)])]
    all_gather x1, waiting for transfers between devices: 21.9 us -> 5.16 us  [on_device(): lax.all_gather(heads, 'blk', axis=0, tiled=True)]
  transfers between devices with their start and end apart: 3 -> 18, of which waited for: 3 -> 10; matrix products, arithmetic and copies ran while one was open for 2% -> 13% of each run, Pallas kernels for 0% -> 39%
where the time goes in v1:
time: 199 us; the launch traced here: 198 us
  Pallas kernels  92.7 us (47%)
  waiting for transfers between devices  31.8 us (16%)
  other arithmetic  20.8 us (10%)
  starting transfers between devices  18.1 us (9%)
  between operations  15 us (8%)
  local copies, waits for them, and re-layouts  9.95 us (5%)
  blocking collectives  8.82 us (4%)
    pallas_call x4, Pallas kernels, tail_chunk(): pl.pallas_call(functools.partial(tail_kernel, first), out_shape=[jax.Shap...  59.9 us
    pallas_call x1, Pallas kernels, head_pass(): pl.pallas_call(head_kernel, out_shape=jax.ShapeDtypeStruct((members, rows...  32.8 us
    ppermute x8, waiting for transfers between devices, on_device(): last = lax.ppermute(onward, 'grp', [(g, g ^ far) for g in range(groups)])  17.7 us
    ppermute x8, starting transfers between devices, on_device(): theirs = lax.ppermute(mine, 'grp', [(g, g ^ near) for g in range(groups)])  9.42 us
    unnamed x1, blocking collectives  8.82 us
    ppermute x8, starting transfers between devices, on_device(): last = lax.ppermute(onward, 'grp', [(g, g ^ far) for g in range(groups)])  8.6 us
    ppermute x8, waiting for transfers between devices, on_device(): theirs = lax.ppermute(mine, 'grp', [(g, g ^ near) for g in range(groups)])  8.31 us
    convert_element_type x8, other arithmetic, on_device(): onward = (take(named(me, me ^ far, at, piece), mine) + take(named(me ^ ne...  8 us
  transfers between devices with their start and end apart: 18, of which 10 were waited for; matrix products, arithmetic and copies ran while one was open for 13% of the time, Pallas kernels for 39%

profile of v1, /device:TPU:0, one launch (start us, length us, event | category | flops | bytes accessed | tf_op | source)
XLA Modules:
  0.0 198.0 jit_solution(11089276927344428263)
XLA Ops:
  15.9 8.8 %all-reduce = s32[64]{0:T(128)S(1)} all-reduce(s32[64]{0:T(128)S(1)} %bitcast_dynamic-update-slice_fusion), channel_id=2, replica_groups=mesh['grp'=4,'blk'=8] {'grp'}, use_global_device_ids=true, to_apply=%add | all-reduce | flops 64 | bytes 512
  25.9 2.7 %fusion.44 = (bf16[512,512]{1,0:T(8,128)(2,1)S(1)}, bf16[512,512]{1,0:T(8,128)(2,1)}, bf16[512,512]{1,0:T(8,128)(2,1)}, bf16[512,512]{1,0:T(8,128)(2,1)}) fusion(bf16[2048,512]{1,0:T(8,128)(2,1)} %param.9), kind=kLoop, calls=%fused_computation.145 | loop fusion | bytes 4194304 | tf_op jit(solution)/shard_map/slice | solution.py:260
  29.4 5.2 %all-gather.3.cloned.1.call-done = bf16[1024,512]{1,0:T(8,128)(2,1)} async-done(((bf16[128,512]{1,0:T(8,128)(2,1)}), bf16[1024,512]{1,0:T(8,128)(2,1)}) %all-gather.3.cloned.1.call-update) | async-done | bytes 1048592 | tf_op jit(solution)/shard_map/all_gather | solution.py:245
  35.8 14.5 %tail_chunk.4 = (bf16[4,128,512]{2,1,0:T(8,128)(2,1)S(1)}, bf16[257,128,128]{2,1,0:T(8,128)(2,1)S(1)}) custom-call(s32[320]{0:T(512)S(1)} %broadcast_add_fusion.list_ref, s32[17]{0:T(128)S(1)} %select_reduce_fusion.4.gs_ref, s32[256]{0:T(256)S(1)} %copy-done.13, bf16[8,128,512]{2,1,0:T(8,128)(2,1)S(1)} %bitcast.76, bf16[4,128,512]{2,1,0:T(8,128)(2,1)S(1)} %bitcast.84, ...), custom_call_target="tpu_custom_call" | custom-call | flops 4294967296 | bytes 6291456 | tf_op jit(solution)/shard_map/tail_chunk/pallas_call | solution.py:190
  52.3 4.5 %collective-permute-start = (bf16[2,128,512]{2,1,0:T(8,128)(2,1)S(1)}, bf16[2,128,512]{2,1,0:T(8,128)(2,1)S(1)}, u32[]{:S(2)}, u32[]{:S(2)}) collective-permute-start(bf16[2,128,512]{2,1,0:T(8,128)(2,1)S(1)} %get-tuple-element.37), channel_id=1, source_target_pairs={{0,8},{8,0},{16,24},{24,16},{1,9},{9,1},{17,25},{25,17},{2,10},{10... | collective-permute-start | bytes 786440 | tf_op jit(solution)/shard_map/ppermute | solution.py:285
  56.8 13.8 %tail_chunk.5 = (bf16[4,128,512]{2,1,0:T(8,128)(2,1)S(1)}, bf16[257,128,128]{2,1,0:T(8,128)(2,1)S(1)}) custom-call(s32[320]{0:T(512)S(1)} %broadcast_add_fusion.list_ref, s32[17]{0:T(128)S(1)} %select_reduce_fusion.4.gs_ref, s32[256]{0:T(256)S(1)} %copy-done.13, bf16[8,128,512]{2,1,0:T(8,128)(2,1)S(1)} %bitcast.77, ...), custom_call_target="tpu_custom_call", output_to_operand_aliasing={{1}: (7, {})} | custom-call | flops 4294967296 | bytes 6291456 | tf_op jit(solution)/shard_map/tail_chunk/pallas_call | solution.py:190
  71.4 14.5 %tail_chunk.6 = (bf16[4,128,512]{2,1,0:T(8,128)(2,1)S(1)}, bf16[257,128,128]{2,1,0:T(8,128)(2,1)S(1)}) custom-call(s32[320]{0:T(512)S(1)} %broadcast_add_fusion.list_ref, s32[17]{0:T(128)S(1)} %select_reduce_fusion.4.gs_ref, s32[256]{0:T(256)S(1)} %copy-done.13, bf16[8,128,512]{2,1,0:T(8,128)(2,1)S(1)} %bitcast.78, ...), custom_call_target="tpu_custom_call", output_to_operand_aliasing={{1}: (7, {})} | custom-call | flops 4294967296 | bytes 6291456 | tf_op jit(solution)/shard_map/tail_chunk/pallas_call | solution.py:190
  86.0 17.0 %tail_chunk.7 = (bf16[4,128,512]{2,1,0:T(8,128)(2,1)S(1)}, bf16[257,128,128]{2,1,0:T(8,128)(2,1)S(1)}) custom-call(s32[320]{0:T(512)S(1)} %broadcast_add_fusion.list_ref, s32[17]{0:T(128)S(1)} %select_reduce_fusion.4.gs_ref, s32[256]{0:T(256)S(1)} %copy-done.13, bf16[8,128,512]{2,1,0:T(8,128)(2,1)S(1)} %bitcast.79, ...), custom_call_target="tpu_custom_call", output_to_operand_aliasing={{1}: (7, {})} | custom-call | flops 4294967296 | bytes 6291456 | tf_op jit(solution)/shard_map/tail_chunk/pallas_call | solution.py:190
  104.8 32.8 %head_pass.1 = bf16[8,128,512]{2,1,0:T(8,128)(2,1)S(1)} custom-call(s32[288]{0:T(512)S(1)} %broadcast_add_fusion.1.list_ref, s32[9]{0:T(128)S(1)} %select_reduce_fusion.5.gs_ref, s32[256]{0:T(256)S(1)} %copy-done.14, bf16[16,128,512]{2,1,0:T(8,128)(2,1)S(1)} %bitcast.80, f32[256,512]{1,0:T(8,128)S(1)} %fusion.rel_ref, ...), custom_call_target="tpu_custom_call" | custom-call | flops 8623489024 | bytes 8421376 | tf_op jit(solution)/shard_map/head_pass/pallas_call | solution.py:219
  139.8 1.3 collective-permute-start.6
  141.2 2.3 %fusion.11 = (bf16[2,128,512]{2,1,0:T(8,128)(2,1)S(1)}, f32[16,128,512]{2,1,0:T(8,128)}) fusion(bf16[2,128,512]{2,1,0:T(8,128)(2,1)} %collective-permute-done.2, pred[2]{0:T(512)(128)(4,1)S(1)} %get-tuple-element.58, pred[2]{0:T(512)(128)(4,1)S(1)} %get-tuple-element.43, bf16[4,128,512]{2,1,0:T(8,128)(2,1)} %copy-done.6, ...), kind=kLoop, calls=%fused_computation.44 | loop fusion | flops 1703935 | bytes 2097160 | tf_op jit(solution)/shard_map/convert_element_type | solution.py:289
  143.6 2.0 %collective-permute-start.3 = (bf16[2,128,512]{2,1,0:T(8,128)(2,1)S(1)}, bf16[2,128,512]{2,1,0:T(8,128)(2,1)S(1)}, u32[]{:S(2)}, u32[]{:S(2)}) collective-permute-start(bf16[2,128,512]{2,1,0:T(8,128)(2,1)S(1)} %get-tuple-element.34), channel_id=1, source_target_pairs={{0,8},{8,0},{16,24},{24,16},{1,9},{9,1},{17,25},{25,17},{2,10},{10... | collective-permute-start | bytes 786440 | tf_op jit(solution)/shard_map/ppermute | solution.py:290
  145.6 4.6 %collective-permute-done.4 = bf16[2,128,512]{2,1,0:T(8,128)(2,1)S(1)} collective-permute-done((bf16[2,128,512]{2,1,0:T(8,128)(2,1)S(1)}, bf16[2,128,512]{2,1,0:T(8,128)(2,1)S(1)}, u32[]{:S(2)}, u32[]{:S(2)}) %collective-permute-start.4) | collective-permute-done | bytes 262176 | tf_op jit(solution)/shard_map/ppermute | solution.py:285
  153.5 2.1 %collective-permute-done.3 = bf16[2,128,512]{2,1,0:T(8,128)(2,1)S(1)} collective-permute-done((bf16[2,128,512]{2,1,0:T(8,128)(2,1)S(1)}, bf16[2,128,512]{2,1,0:T(8,128)(2,1)S(1)}, u32[]{:S(2)}, u32[]{:S(2)}) %collective-permute-start.3) | collective-permute-done | bytes 262176 | tf_op jit(solution)/shard_map/ppermute | solution.py:290
  155.6 1.9 fusion.9
  158.8 3.7 %collective-permute-done.8 = bf16[2,128,512]{2,1,0:T(8,128)(2,1)S(1)} collective-permute-done((bf16[2,128,512]{2,1,0:T(8,128)(2,1)S(1)}, bf16[2,128,512]{2,1,0:T(8,128)(2,1)S(1)}, u32[]{:S(2)}, u32[]{:S(2)}) %collective-permute-start.8) | collective-permute-done | bytes 262176 | tf_op jit(solution)/shard_map/ppermute | solution.py:285
  164.1 2.9 %collective-permute-done.7 = bf16[2,128,512]{2,1,0:T(8,128)(2,1)S(1)} collective-permute-done((bf16[2,128,512]{2,1,0:T(8,128)(2,1)S(1)}, bf16[2,128,512]{2,1,0:T(8,128)(2,1)S(1)}, u32[]{:S(2)}, u32[]{:S(2)}) %collective-permute-start.7) | collective-permute-done | bytes 262176 | tf_op jit(solution)/shard_map/ppermute | solution.py:290
  168.0 2.9 %collective-permute-done.9 = bf16[2,128,512]{2,1,0:T(8,128)(2,1)S(1)} collective-permute-done((bf16[2,128,512]{2,1,0:T(8,128)(2,1)S(1)}, bf16[2,128,512]{2,1,0:T(8,128)(2,1)S(1)}, u32[]{:S(2)}, u32[]{:S(2)}) %collective-permute-start.9) | collective-permute-done | bytes 262176 | tf_op jit(solution)/shard_map/ppermute | solution.py:290
  173.4 1.5 collective-permute-start.13
  174.9 3.4 %collective-permute-done.11 = bf16[2,128,512]{2,1,0:T(8,128)(2,1)S(1)} collective-permute-done((bf16[2,128,512]{2,1,0:T(8,128)(2,1)S(1)}, bf16[2,128,512]{2,1,0:T(8,128)(2,1)S(1)}, u32[]{:S(2)}, u32[]{:S(2)}) %collective-permute-start.11) | collective-permute-done | bytes 262176 | tf_op jit(solution)/shard_map/ppermute | solution.py:290
  179.3 1.8 collective-permute-done.13
  182.2 2.0 %collective-permute-start.15 = (bf16[2,128,512]{2,1,0:T(8,128)(2,1)S(1)}, bf16[2,128,512]{2,1,0:T(8,128)(2,1)S(1)}, u32[]{:S(2)}, u32[]{:S(2)}) collective-permute-start(bf16[2,128,512]{2,1,0:T(8,128)(2,1)S(1)} %get-tuple-element.22), channel_id=1, source_target_pairs={{0,8},{8,0},{16,24},{24,16},{1,9},{9,1},{17,25},{25,17},{2,10},{10... | collective-permute-start | bytes 786440 | tf_op jit(solution)/shard_map/ppermute | solution.py:290
  184.2 4.3 %collective-permute-done.15 = bf16[2,128,512]{2,1,0:T(8,128)(2,1)S(1)} collective-permute-done((bf16[2,128,512]{2,1,0:T(8,128)(2,1)S(1)}, bf16[2,128,512]{2,1,0:T(8,128)(2,1)S(1)}, u32[]{:S(2)}, u32[]{:S(2)}) %collective-permute-start.15) | collective-permute-done | bytes 262176 | tf_op jit(solution)/shard_map/ppermute | solution.py:290
  189.5 1.6 convert_element_type.132
  (99 shorter events, 30.6 us)
Async XLA Ops:
  7.2 21.4 %copy-start = (bf16[2304,512]{1,0:T(8,128)(2,1)S(1)}, bf16[2304,512]{1,0:T(8,128)(2,1)}, u32[]{:S(2)}) copy-start(bf16[2304,512]{1,0:T(8,128)(2,1)} %param.10) | copy-start | bytes 7077892
  7.2 27.4 %all-gather.3.cloned.1.call-start = ((), (), s32[]{:S(2)}) async-start(), calls=%async_computation.1 | async-start | bytes 1179648 | tf_op jit(solution)/shard_map/all_gather | solution.py:245
  7.9 181.6 %reduce-scatter.2.cloned.1.call-start = ((), (), s32[]{:S(2)}) async-start(), calls=%async_computation.2 | async-start | bytes 1179648 | tf_op jit(solution)/shard_map/reduce_scatter | solution.py:265
  35.8 21.0 %copy-start.11 = (bf16[512,512]{1,0:T(8,128)(2,1)S(1)}, bf16[512,512]{1,0:T(8,128)(2,1)}, u32[]{:S(2)}) copy-start(bf16[512,512]{1,0:T(8,128)(2,1)} %get-tuple-element.21) | copy-start | bytes 1572868
  50.3 52.8 %copy-start.6 = (bf16[4,128,512]{2,1,0:T(8,128)(2,1)}, bf16[4,128,512]{2,1,0:T(8,128)(2,1)S(1)}, u32[]{:S(2)}) copy-start(bf16[4,128,512]{2,1,0:T(8,128)(2,1)S(1)} %get-tuple-element.14) | copy-start | bytes 1572868
  51.1 90.1 %collective-permute-start.2 = (bf16[2,128,512]{2,1,0:T(8,128)(2,1)}, bf16[2,128,512]{2,1,0:T(8,128)(2,1)}, u32[]{:S(2)}, u32[]{:S(2)}) collective-permute-start(bf16[2,128,512]{2,1,0:T(8,128)(2,1)} %get-tuple-element.36), channel_id=1, source_target_pairs={{0,16},{8,24},{16,0},{24,8},{1,17},{9,25},{17,1},{25,9},{2,18},{10... | collective-permute-start | bytes 786440 | tf_op jit(solution)/shard_map/ppermute | solution.py:285
  52.3 50.8 %collective-permute-start = (bf16[2,128,512]{2,1,0:T(8,128)(2,1)S(1)}, bf16[2,128,512]{2,1,0:T(8,128)(2,1)S(1)}, u32[]{:S(2)}, u32[]{:S(2)}) collective-permute-start(bf16[2,128,512]{2,1,0:T(8,128)(2,1)S(1)} %get-tuple-element.37), channel_id=1, source_target_pairs={{0,8},{8,0},{16,24},{24,16},{1,9},{9,1},{17,25},{25,17},{2,10},{10... | collective-permute-start | bytes 786440 | tf_op jit(solution)/shard_map/ppermute | solution.py:285
  86.0 18.8 %copy-start.8 = (bf16[2048,512]{1,0:T(8,128)(2,1)S(1)}, bf16[2048,512]{1,0:T(8,128)(2,1)}, u32[]{:S(2)}) copy-start(bf16[2048,512]{1,0:T(8,128)(2,1)} %param.9) | copy-start | bytes 6291460
  103.1 34.5 %copy-start.15 = (bf16[2,128,512]{2,1,0:T(8,128)(2,1)}, bf16[2,128,512]{2,1,0:T(8,128)(2,1)S(1)}, u32[]{:S(2)}) copy-start(bf16[2,128,512]{2,1,0:T(8,128)(2,1)S(1)} %collective-permute-done) | copy-start | bytes 786436
  104.0 37.2 %collective-permute-start.1 = (bf16[2,128,512]{2,1,0:T(8,128)(2,1)}, bf16[2,128,512]{2,1,0:T(8,128)(2,1)}, u32[]{:S(2)}, u32[]{:S(2)}) collective-permute-start(bf16[2,128,512]{2,1,0:T(8,128)(2,1)} %fusion.6), channel_id=1, source_target_pairs={{0,16},{8,24},{16,0},{24,8},{1,17},{9,25},{17,1},{25,9},{2,18},{10... | collective-permute-start | bytes 786440 | tf_op jit(solution)/shard_map/ppermute | solution.py:290
  138.7 19.1 %copy-start.5 = (bf16[4,128,512]{2,1,0:T(8,128)(2,1)S(1)}, bf16[4,128,512]{2,1,0:T(8,128)(2,1)}, u32[]{:S(2)}) copy-start(bf16[4,128,512]{2,1,0:T(8,128)(2,1)} %copy-done.4) | copy-start | bytes 1572868
  139.8 17.7 %collective-permute-start.6 = (bf16[2,128,512]{2,1,0:T(8,128)(2,1)S(1)}, bf16[2,128,512]{2,1,0:T(8,128)(2,1)S(1)}, u32[]{:S(2)}, u32[]{:S(2)}) collective-permute-start(bf16[2,128,512]{2,1,0:T(8,128)(2,1)S(1)} %get-tuple-element.32), channel_id=1, source_target_pairs={{0,16},{8,24},{16,0},{24,8},{1,17},{9,25},{17,1},{25,9},{2,18},{10... | collective-permute-start | bytes 786440 | tf_op jit(solution)/shard_map/ppermute | solution.py:285
  141.2 8.9 %collective-permute-start.4 = (bf16[2,128,512]{2,1,0:T(8,128)(2,1)S(1)}, bf16[2,128,512]{2,1,0:T(8,128)(2,1)S(1)}, u32[]{:S(2)}, u32[]{:S(2)}) collective-permute-start(bf16[2,128,512]{2,1,0:T(8,128)(2,1)S(1)} %get-tuple-element.33), channel_id=1, source_target_pairs={{0,8},{8,0},{16,24},{24,16},{1,9},{9,1},{17,25},{25,17},{2,10},{10... | collective-permute-start | bytes 786440 | tf_op jit(solution)/shard_map/ppermute | solution.py:285
  143.6 12.0 %collective-permute-start.3 = (bf16[2,128,512]{2,1,0:T(8,128)(2,1)S(1)}, bf16[2,128,512]{2,1,0:T(8,128)(2,1)S(1)}, u32[]{:S(2)}, u32[]{:S(2)}) collective-permute-start(bf16[2,128,512]{2,1,0:T(8,128)(2,1)S(1)} %get-tuple-element.34), channel_id=1, source_target_pairs={{0,8},{8,0},{16,24},{24,16},{1,9},{9,1},{17,25},{25,17},{2,10},{10... | collective-permute-start | bytes 786440 | tf_op jit(solution)/shard_map/ppermute | solution.py:290
  151.3 6.4 %collective-permute-start.5 = (bf16[2,128,512]{2,1,0:T(8,128)(2,1)S(1)}, bf16[2,128,512]{2,1,0:T(8,128)(2,1)S(1)}, u32[]{:S(2)}, u32[]{:S(2)}) collective-permute-start(bf16[2,128,512]{2,1,0:T(8,128)(2,1)S(1)} %fusion.16), channel_id=1, source_target_pairs={{0,16},{8,24},{16,0},{24,8},{1,17},{9,25},{17,1},{25,9},{2,18},{10... | collective-permute-start | bytes 786440 | tf_op jit(solution)/shard_map/ppermute | solution.py:290
  152.4 15.5 %collective-permute-start.10 = (bf16[2,128,512]{2,1,0:T(8,128)(2,1)S(1)}, bf16[2,128,512]{2,1,0:T(8,128)(2,1)S(1)}, u32[]{:S(2)}, u32[]{:S(2)}) collective-permute-start(bf16[2,128,512]{2,1,0:T(8,128)(2,1)S(1)} %get-tuple-element.28), channel_id=1, source_target_pairs={{0,16},{8,24},{16,0},{24,8},{1,17},{9,25},{17,1},{25,9},{2,18},{10... | collective-permute-start | bytes 786440 | tf_op jit(solution)/shard_map/ppermute | solution.py:285
  153.5 9.1 %collective-permute-start.8 = (bf16[2,128,512]{2,1,0:T(8,128)(2,1)S(1)}, bf16[2,128,512]{2,1,0:T(8,128)(2,1)S(1)}, u32[]{:S(2)}, u32[]{:S(2)}) collective-permute-start(bf16[2,128,512]{2,1,0:T(8,128)(2,1)S(1)} %get-tuple-element.29), channel_id=1, source_target_pairs={{0,8},{8,0},{16,24},{24,16},{1,9},{9,1},{17,25},{25,17},{2,10},{10... | collective-permute-start | bytes 786440 | tf_op jit(solution)/shard_map/ppermute | solution.py:285
  158.8 8.2 %collective-permute-start.7 = (bf16[2,128,512]{2,1,0:T(8,128)(2,1)S(1)}, bf16[2,128,512]{2,1,0:T(8,128)(2,1)S(1)}, u32[]{:S(2)}, u32[]{:S(2)}) collective-permute-start(bf16[2,128,512]{2,1,0:T(8,128)(2,1)S(1)} %get-tuple-element.30), channel_id=1, source_target_pairs={{0,8},{8,0},{16,24},{24,16},{1,9},{9,1},{17,25},{25,17},{2,10},{10... | collective-permute-start | bytes 786440 | tf_op jit(solution)/shard_map/ppermute | solution.py:290
  162.7 8.1 %collective-permute-start.9 = (bf16[2,128,512]{2,1,0:T(8,128)(2,1)S(1)}, bf16[2,128,512]{2,1,0:T(8,128)(2,1)S(1)}, u32[]{:S(2)}, u32[]{:S(2)}) collective-permute-start(bf16[2,128,512]{2,1,0:T(8,128)(2,1)S(1)} %fusion.26), channel_id=1, source_target_pairs={{0,16},{8,24},{16,0},{24,8},{1,17},{9,25},{17,1},{25,9},{2,18},{10... | collective-permute-start | bytes 786440 | tf_op jit(solution)/shard_map/ppermute | solution.py:290
  164.0 9.2 %collective-permute-start.12 = (bf16[2,128,512]{2,1,0:T(8,128)(2,1)S(1)}, bf16[2,128,512]{2,1,0:T(8,128)(2,1)S(1)}, u32[]{:S(2)}, u32[]{:S(2)}) collective-permute-start(bf16[2,128,512]{2,1,0:T(8,128)(2,1)S(1)} %get-tuple-element.25), channel_id=1, source_target_pairs={{0,8},{8,0},{16,24},{24,16},{1,9},{9,1},{17,25},{25,17},{2,10},{10... | collective-permute-start | bytes 786440 | tf_op jit(solution)/shard_map/ppermute | solution.py:285
  171.9 6.4 %collective-permute-start.11 = (bf16[2,128,512]{2,1,0:T(8,128)(2,1)S(1)}, bf16[2,128,512]{2,1,0:T(8,128)(2,1)S(1)}, u32[]{:S(2)}, u32[]{:S(2)}) collective-permute-start(bf16[2,128,512]{2,1,0:T(8,128)(2,1)S(1)} %get-tuple-element.26), channel_id=1, source_target_pairs={{0,8},{8,0},{16,24},{24,16},{1,9},{9,1},{17,25},{25,17},{2,10},{10... | collective-permute-start | bytes 786440 | tf_op jit(solution)/shard_map/ppermute | solution.py:290
  171.9 7.4 %collective-permute-start.14 = (bf16[2,128,512]{2,1,0:T(8,128)(2,1)S(1)}, bf16[2,128,512]{2,1,0:T(8,128)(2,1)S(1)}, u32[]{:S(2)}, u32[]{:S(2)}) collective-permute-start(bf16[2,128,512]{2,1,0:T(8,128)(2,1)S(1)} %get-tuple-element.24), channel_id=1, source_target_pairs={{0,16},{8,24},{16,0},{24,8},{1,17},{9,25},{17,1},{25,9},{2,18},{10... | collective-permute-start | bytes 786440 | tf_op jit(solution)/shard_map/ppermute | solution.py:285
  173.4 7.7 %collective-permute-start.13 = (bf16[2,128,512]{2,1,0:T(8,128)(2,1)S(1)}, bf16[2,128,512]{2,1,0:T(8,128)(2,1)S(1)}, u32[]{:S(2)}, u32[]{:S(2)}) collective-permute-start(bf16[2,128,512]{2,1,0:T(8,128)(2,1)S(1)} %fusion.36), channel_id=1, source_target_pairs={{0,16},{8,24},{16,0},{24,8},{1,17},{9,25},{17,1},{25,9},{2,18},{10... | collective-permute-start | bytes 786440 | tf_op jit(solution)/shard_map/ppermute | solution.py:290
  182.2 6.4 %collective-permute-start.15 = (bf16[2,128,512]{2,1,0:T(8,128)(2,1)S(1)}, bf16[2,128,512]{2,1,0:T(8,128)(2,1)S(1)}, u32[]{:S(2)}, u32[]{:S(2)}) collective-permute-start(bf16[2,128,512]{2,1,0:T(8,128)(2,1)S(1)} %get-tuple-element.22), channel_id=1, source_target_pairs={{0,8},{8,0},{16,24},{24,16},{1,9},{9,1},{17,25},{25,17},{2,10},{10... | collective-permute-start | bytes 786440 | tf_op jit(solution)/shard_map/ppermute | solution.py:290
  (12 other events, 128.3 us)
Sparse Core Ops, SparseCore 0:
  9.6 24.9 all-gather.2
  138.8 30.6 reduce-scatter.1

commit v2 on v1

--- a/solution.py
+++ b/solution.py
@@ -8,9 +8,9 @@
 from jax.sharding import PartitionSpec as P
 
 grad_scale = 0.125
-GROUP = 4
+GROUP = 8
 DEPTH = 4
-CHUNKS = 4
+CHUNKS = 2
 
 
 def group_lists(names, kinds, size):
@@ -114,10 +114,11 @@
             settle(lax.rem(steps - back, 2))
 
 
-def head_kernel(list_ref, gs_ref, tb_ref, tails_ref, rel_ref, slope_ref, head_out, buf, acc, sem):
+def head_kernel(first, list_ref, gs_ref, tb_ref, tails_ref, rel_ref, slope_ref, head_out, buf, acc, sem):
     members = head_out.shape[0]
     half = tails_ref.shape[2] // 2
-    end = gs_ref[members]
+    begin = gs_ref[first]
+    end = gs_ref[first + members]
 
     def fetch(j, slot):
         for g in range(GROUP):
@@ -125,16 +126,17 @@
             pltpu.make_async_copy(slope_ref.at[k], buf.at[slot, g], sem.at[slot, g]).start()
 
     for d in range(DEPTH - 1):
-        @pl.when(d < end)
-        def _():
-            fetch(d, d)
+        @pl.when(begin + d < end)
+        def _():
+            fetch(begin + d, d)
 
     def body(j):
-        slot = lax.rem(j, DEPTH)
+        step = j - begin
+        slot = lax.rem(step, DEPTH)
 
         @pl.when(j + DEPTH - 1 < end)
         def _():
-            fetch(j + DEPTH - 1, lax.rem(j + DEPTH - 1, DEPTH))
+            fetch(j + DEPTH - 1, lax.rem(step + DEPTH - 1, DEPTH))
 
         for g in range(GROUP):
             pltpu.make_async_copy(slope_ref.at[0], buf.at[slot, g], sem.at[slot, g]).wait()
@@ -164,7 +166,7 @@
             body(j)
             return c
 
-        lax.fori_loop(gs_ref[h], gs_ref[h + 1], inner, 0)
+        lax.fori_loop(gs_ref[first + h], gs_ref[first + h + 1], inner, 0)
         head_out[h] = acc[...].astype(jnp.bfloat16)
         return carry
 
@@ -205,7 +207,7 @@
         input_output_aliases=aliases,
         compiler_params=pltpu.CompilerParams(vmem_limit_bytes=32 * 1024 * 1024),
         cost_estimate=pl.CostEstimate(
-            flops=8 * work * rows * rows * width,
+            flops=26 * work * rows * rows * width,
             bytes_accessed=work * rows * rows * 6,
             transcendentals=work * rows * rows,
         ),
@@ -213,11 +215,11 @@
     )(*args)
 
 
-def head_pass(members, listing, starts, tb, tails, rel, slopes):
+def head_pass(first, members, share, listing, starts, tb, tails, rel, slopes):
     _, rows, width = tails.shape
-    work = slopes.shape[0]
+    work = slopes.shape[0] // share
     return pl.pallas_call(
-        head_kernel,
+        functools.partial(head_kernel, first),
         out_shape=jax.ShapeDtypeStruct((members, rows, width), jnp.bfloat16),
         in_specs=[smem, smem, smem, vmem, vmem, hbm],
         out_specs=vmem,
@@ -228,7 +230,7 @@
         ],
         compiler_params=pltpu.CompilerParams(vmem_limit_bytes=32 * 1024 * 1024),
         cost_estimate=pl.CostEstimate(
-            flops=4 * work * rows * rows * width,
+            flops=16 * work * rows * rows * width,
             bytes_accessed=work * rows * rows * 2,
             transcendentals=0,
         ),
@@ -261,11 +263,6 @@
         )
         parts.append(part)
 
-    head_local = head_pass(members, by_head, head_starts, tail_block, tails3, rel, slopes)
-    head_grad = lax.psum_scatter(
-        head_local.reshape(members * rows, width), "blk", scatter_dimension=0, tiled=True
-    ).astype(jnp.float32)
-
     def named(source, target, at, count):
         route = lax.dynamic_slice_in_dim(
             lax.dynamic_index_in_dim(owners, source, 0, keepdims=False), at, count
@@ -276,23 +273,47 @@
         return jnp.where(mask, value.astype(jnp.float32), 0.0)
 
     piece = own // 2
-    outs = []
+    kept, onwards = [], []
     for c in range(CHUNKS):
         for side in range(2):
             near, far = (1, 2) if side == 0 else (2, 1)
             at = c * own + side * piece
             mine = parts[c][side * piece : (side + 1) * piece]
             theirs = lax.ppermute(mine, "grp", [(g, g ^ near) for g in range(groups)])
-            onward = (
-                take(named(me, me ^ far, at, piece), mine)
-                + take(named(me ^ near, me ^ far, at, piece), theirs)
-            ).astype(jnp.bfloat16)
-            last = lax.ppermute(onward, "grp", [(g, g ^ far) for g in range(groups)])
-            outs.append(
-                take(named(me, me, at, piece), mine)
-                + take(named(me ^ near, me, at, piece), theirs)
-                + last.astype(jnp.float32)
+            onwards.append(
+                (
+                    take(named(me, me ^ far, at, piece), mine)
+                    + take(named(me ^ near, me ^ far, at, piece), theirs)
+                ).astype(jnp.bfloat16)
             )
+            kept.append((near, far, at, mine, theirs))
+
+    def onward_step(i, value):
+        far = kept[i][1]
+        return lax.ppermute(value, "grp", [(g, g ^ far) for g in range(groups)])
+
+    early = 2 * (CHUNKS - 1)
+    part = members // 2
+    slopes, *onwards[:early] = lax.optimization_barrier((slopes, *onwards[:early]))
+    lasts = [onward_step(i, v) for i, v in enumerate(onwards[:early])]
+    low = head_pass(0, part, 2, by_head, head_starts, tail_block, tails3, rel, slopes)
+    slopes, low, lasts, onwards = lax.optimization_barrier((slopes, low, lasts, onwards))
+    lasts = lasts + [onward_step(i, onwards[i]) for i in range(early, len(onwards))]
+    high = head_pass(
+        part, members - part, 2, by_head, head_starts, tail_block, tails3, rel, slopes
+    )
+    head_local = jnp.concatenate([low, high], axis=0)
+    head_grad = lax.psum_scatter(
+        head_local.reshape(members * rows, width), "blk", scatter_dimension=0, tiled=True
+    ).astype(jnp.float32)
+
+    outs = []
+    for last, (near, far, at, mine, theirs) in zip(lasts, kept):
+        outs.append(
+            take(named(me, me, at, piece), mine)
+            + take(named(me ^ near, me, at, piece), theirs)
+            + last.astype(jnp.float32)
+        )
     tail_grad = jnp.concatenate(outs, axis=0).reshape(blocks * rows, width)
     return (head_grad, tail_grad)
 

time: 199 us -> 173 us (0.87)
  Pallas kernels: 92.7 us -> 78.5 us
  other arithmetic: 20.8 us -> 16.2 us
  local copies, waits for them, and re-layouts: 9.95 us -> 5.71 us
  starting transfers between devices: 18.1 us -> 14.6 us
    reduce_scatter x1, waiting for transfers between devices: 0.01 us -> 14.6 us  [on_device(): lax.psum_scatter(head_local.reshape(members * rows, width), 'blk', scatte...]
    pallas_call x4 -> x2, Pallas kernels: 59.9 us -> 50.2 us  [tail_chunk(): pl.pallas_call(functools.partial(tail_kernel, first), out_shape=[jax.Shap...]
    ppermute x8 -> x4, waiting for transfers between devices: 8.31 us -> 0.01 us  [on_device(): theirs = lax.ppermute(mine, 'grp', [(g, g ^ near) for g in range(groups)])]
    ppermute x8 -> x4, waiting for transfers between devices: 17.7 us -> 10.6 us  [onward_step(): return lax.ppermute(value, 'grp', [(g, g ^ far) for g in range(groups)])]
    convert_element_type x8 -> x2, other arithmetic: 8 us -> 2.06 us  [on_device(): onwards.append((take(named(me, me ^ far, at, piece), mine) + take(named(m...]
    pallas_call x1 -> x2, Pallas kernels: 32.8 us -> 28.3 us  [head_pass(): pl.pallas_call(functools.partial(head_kernel, first), out_shape=jax.Shape...]
    unnamed x3 -> x0, other arithmetic: 3.9 us -> none
    add x0 -> x2, other arithmetic: none -> 3.08 us  [on_device(): take(named(me, me, at, piece), mine)]
  transfers between devices with their start and end apart: 18 -> 10, of which waited for: 10 -> 6; matrix products, arithmetic and copies ran while one was open for 13% -> 11% of each run, Pallas kernels for 39% -> 24%
where the time goes in v2:
time: 173 us
  Pallas kernels  78.5 us (45%)
  waiting for transfers between devices  31.5 us (18%)
  other arithmetic  16.2 us (9%)
  between operations  15 us (9%)
  starting transfers between devices  14.6 us (8%)
  blocking collectives  8.82 us (5%)
  local copies, waits for them, and re-layouts  5.71 us (3%)
  matrix products  2.51 us (1%)
    pallas_call x2, Pallas kernels, tail_chunk(): pl.pallas_call(functools.partial(tail_kernel, first), out_shape=[jax.Shap...  50.2 us
    pallas_call x2, Pallas kernels, head_pass(): pl.pallas_call(functools.partial(head_kernel, first), out_shape=jax.Shape...  28.3 us
    reduce_scatter x1, waiting for transfers between devices, on_device(): lax.psum_scatter(head_local.reshape(members * rows, width), 'blk', scatte...  14.6 us
    ppermute x4, waiting for transfers between devices, onward_step(): return lax.ppermute(value, 'grp', [(g, g ^ far) for g in range(groups)])  10.6 us
    unnamed x1, blocking collectives  8.82 us
    ppermute x4, starting transfers between devices, on_device(): theirs = lax.ppermute(mine, 'grp', [(g, g ^ near) for g in range(groups)])  7.54 us
    ppermute x4, starting transfers between devices, onward_step(): return lax.ppermute(value, 'grp', [(g, g ^ far) for g in range(groups)])  6.96 us
    all_gather x1, waiting for transfers between devices, on_device(): lax.all_gather(heads, 'blk', axis=0, tiled=True)  5.59 us
  transfers between devices with their start and end apart: 10, of which 6 were waited for; matrix products, arithmetic and copies ran while one was open for 11% of the time, Pallas kernels for 24%

profile of v2, /device:TPU:0, one launch (start us, length us, event | category | flops | bytes accessed | tf_op | source)
XLA Modules:
  0.0 172.8 jit_solution(1268432280037267558)
XLA Ops:
  13.2 1.2 dynamic-slice
  15.9 8.8 %all-reduce = s32[64]{0:T(128)S(1)} all-reduce(s32[64]{0:T(128)S(1)} %bitcast_dynamic-update-slice_fusion), channel_id=2, replica_groups=mesh['grp'=4,'blk'=8] {'grp'}, use_global_device_ids=true, to_apply=%add | all-reduce | flops 64 | bytes 512
  25.3 2.5 %fusion.rel_ref = f32[256,512]{1,0:T(8,128)} fusion(bf16[2304,512]{1,0:T(8,128)(2,1)S(1)} %copy-done, s32[256]{0:T(256)} %param.13), kind=kOutput, calls=%fused_computation.2 | convolution fusion | flops 604569600 | bytes 2884608 | tf_op jit(solution)/shard_map/dot_general | solution.py:252
  27.8 1.1 fusion.20
  28.9 5.6 %all-gather.3.cloned.1.call-done = bf16[1024,512]{1,0:T(8,128)(2,1)} async-done(((bf16[128,512]{1,0:T(8,128)(2,1)}), bf16[1024,512]{1,0:T(8,128)(2,1)}) %all-gather.3.cloned.1.call-update) | async-done | bytes 1048592 | tf_op jit(solution)/shard_map/all_gather | solution.py:247
  34.5 1.2 copy-done.7
  36.8 23.2 %tail_chunk.2 = (bf16[8,128,512]{2,1,0:T(8,128)(2,1)S(1)}, bf16[257,128,128]{2,1,0:T(8,128)(2,1)S(1)}) custom-call(s32[384]{0:T(512)S(1)} %broadcast_add_fusion.1.list_ref, s32[17]{0:T(128)S(1)} %select_reduce_fusion.4.gs_ref, s32[256]{0:T(256)S(1)} %copy-done.5, bf16[8,128,512]{2,1,0:T(8,128)(2,1)S(1)} %bitcast.46, bf16[8,128,512]{2,1,0:T(8,128)(2,1)S(1)} %bitcast.45, ...), custom_call_target="tpu_custom_call" | custom-call | flops 27917287424 | bytes 12582912 | tf_op jit(solution)/shard_map/tail_chunk/pallas_call | solution.py:192
  60.1 2.3 %collective-permute-start.1 = (bf16[4,128,512]{2,1,0:T(8,128)(2,1)S(1)}, bf16[4,128,512]{2,1,0:T(8,128)(2,1)S(1)}, u32[]{:S(2)}, u32[]{:S(2)}) collective-permute-start(bf16[4,128,512]{2,1,0:T(8,128)(2,1)S(1)} %get-tuple-element.40), channel_id=1, source_target_pairs={{0,16},{8,24},{16,0},{24,8},{1,17},{9,25},{17,1},{25,9},{2,18},{10... | collective-permute-start | bytes 1572872 | tf_op jit(solution)/shard_map/ppermute | solution.py:282
  62.5 5.0 %collective-permute-start = (bf16[4,128,512]{2,1,0:T(8,128)(2,1)S(1)}, bf16[4,128,512]{2,1,0:T(8,128)(2,1)S(1)}, u32[]{:S(2)}, u32[]{:S(2)}) collective-permute-start(bf16[4,128,512]{2,1,0:T(8,128)(2,1)S(1)} %get-tuple-element.41), channel_id=1, source_target_pairs={{0,8},{8,0},{16,24},{24,16},{1,9},{9,1},{17,25},{25,17},{2,10},{10... | collective-permute-start | bytes 1572872 | tf_op jit(solution)/shard_map/ppermute | solution.py:282
  67.5 27.0 %tail_chunk.3 = (bf16[8,128,512]{2,1,0:T(8,128)(2,1)S(1)}, bf16[257,128,128]{2,1,0:T(8,128)(2,1)S(1)}) custom-call(s32[384]{0:T(512)S(1)} %broadcast_add_fusion.1.list_ref, s32[17]{0:T(128)S(1)} %select_reduce_fusion.4.gs_ref, s32[256]{0:T(256)S(1)} %copy-done.5, bf16[8,128,512]{2,1,0:T(8,128)(2,1)S(1)} %bitcast.47, ...), custom_call_target="tpu_custom_call", output_to_operand_aliasing={{1}: (7, {})} | custom-call | flops 27917287424 | bytes 12582912 | tf_op jit(solution)/shard_map/tail_chunk/pallas_call | solution.py:192
  95.4 2.0 %collective-permute-start.2 = (bf16[4,128,512]{2,1,0:T(8,128)(2,1)S(1)}, bf16[4,128,512]{2,1,0:T(8,128)(2,1)S(1)}, u32[]{:S(2)}, u32[]{:S(2)}) collective-permute-start(bf16[4,128,512]{2,1,0:T(8,128)(2,1)S(1)} %get-tuple-element.19), channel_id=1, source_target_pairs={{0,16},{8,24},{16,0},{24,8},{1,17},{9,25},{17,1},{25,9},{2,18},{10... | collective-permute-start | bytes 1572872 | tf_op jit(solution)/shard_map/ppermute | solution.py:293
  97.4 2.0 %collective-permute-start.3 = (bf16[4,128,512]{2,1,0:T(8,128)(2,1)S(1)}, bf16[4,128,512]{2,1,0:T(8,128)(2,1)S(1)}, u32[]{:S(2)}, u32[]{:S(2)}) collective-permute-start(bf16[4,128,512]{2,1,0:T(8,128)(2,1)S(1)} %get-tuple-element.20), channel_id=1, source_target_pairs={{0,8},{8,0},{16,24},{24,16},{1,9},{9,1},{17,25},{25,17},{2,10},{10... | collective-permute-start | bytes 1572872 | tf_op jit(solution)/shard_map/ppermute | solution.py:293
  99.4 14.5 %head_pass.2 = bf16[4,128,512]{2,1,0:T(8,128)(2,1)S(1)} custom-call(s32[320]{0:T(512)S(1)} %broadcast_add_fusion.list_ref, s32[9]{0:T(128)S(1)} %select_reduce_fusion.5.gs_ref, s32[256]{0:T(256)S(1)} %copy-done.6, bf16[16,128,512]{2,1,0:T(8,128)(2,1)S(1)} %bitcast.42, f32[256,512]{1,0:T(8,128)S(1)} %copy-done.8, ...), custom_call_target="tpu_custom_call" | custom-call | flops 17179869184 | bytes 4194304 | tf_op jit(solution)/shard_map/head_pass/pallas_call | solution.py:221
  114.0 1.5 fusion.15
  115.5 1.6 collective-permute-done.2
  117.1 1.5 collective-permute-done.3
  118.6 13.8 %head_pass.3 = bf16[4,128,512]{2,1,0:T(8,128)(2,1)S(1)} custom-call(s32[320]{0:T(512)S(1)} %broadcast_add_fusion.list_ref, s32[9]{0:T(128)S(1)} %select_reduce_fusion.5.gs_ref, s32[256]{0:T(256)S(1)} %copy-done.6, bf16[16,128,512]{2,1,0:T(8,128)(2,1)S(1)} %bitcast.43, f32[256,512]{1,0:T(8,128)S(1)} %copy-done.8, ...), custom_call_target="tpu_custom_call" | custom-call | flops 17179869184 | bytes 4194304 | tf_op jit(solution)/shard_map/head_pass/pallas_call | solution.py:221
  132.4 1.1 pad_maximum_fusion.1
  133.5 2.7 %collective-permute-start.6 = (bf16[4,128,512]{2,1,0:T(8,128)(2,1)}, bf16[4,128,512]{2,1,0:T(8,128)(2,1)S(1)}, u32[]{:S(2)}, u32[]{:S(2)}) collective-permute-start(bf16[4,128,512]{2,1,0:T(8,128)(2,1)} %get-tuple-element.26), channel_id=1, source_target_pairs={{0,16},{8,24},{16,0},{24,8},{1,17},{9,25},{17,1},{25,9},{2,18},{10... | collective-permute-start | bytes 1572872 | tf_op jit(solution)/shard_map/ppermute | solution.py:293
  136.5 2.5 %fusion.5 = (f32[4,128,512]{2,1,0:T(8,128)S(1)}, f32[4,128,512]{2,1,0:T(8,128)S(1)}) fusion(bf16[4,128,512]{2,1,0:T(8,128)(2,1)} %copy-done.12, bf16[4,128,512]{2,1,0:T(8,128)(2,1)} %copy-done.15, pred[4]{0:T(512)(128)(4,1)S(1)} %get-tuple-element.66, pred[4]{0:T(512)(128)(4,1)S(1)} %get-tuple-element.45, bf16[8,128,512]{2,1,0:T(8,128)(2,1)} %copy-done.1, ...), kind=kLoop, calls=%fused_computation.23 | loop fusion | flops 3670016 | bytes 5242896 | tf_op jit(solution)/shard_map/add | solution.py:313
  139.0 7.2 %collective-permute-done.6 = bf16[4,128,512]{2,1,0:T(8,128)(2,1)S(1)} collective-permute-done((bf16[4,128,512]{2,1,0:T(8,128)(2,1)}, bf16[4,128,512]{2,1,0:T(8,128)(2,1)S(1)}, u32[]{:S(2)}, u32[]{:S(2)}) %collective-permute-start.6) | collective-permute-done | bytes 524320 | tf_op jit(solution)/shard_map/ppermute | solution.py:293
  147.1 2.6 %pad_maximum_fusion = f32[16,128,512]{2,1,0:T(8,128)} fusion(f32[4,128,512]{2,1,0:T(8,128)S(1)} %get-tuple-element.33, f32[4,128,512]{2,1,0:T(8,128)S(1)} %get-tuple-element.32, f32[4,128,512]{2,1,0:T(8,128)S(1)} %get-tuple-element.31, f32[4,128,512]{2,1,0:T(8,128)S(1)} %get-tuple-element.30), kind=kLoop, calls=%fused_computation | loop fusion | flops 3145728 | bytes 8388608 | tf_op jit(solution)/shard_map/concatenate | solution.py:317
  149.8 14.6 %reduce-scatter.2.cloned.1.call-done = bf16[128,512]{1,0:T(8,128)(2,1)} async-done(((bf16[1024,512]{1,0:T(8,128)(2,1)}), bf16[128,512]{1,0:T(8,128)(2,1)}) %reduce-scatter.2.cloned.1.call-update) | async-done | bytes 131088 | tf_op jit(solution)/shard_map/reduce_scatter | solution.py:306
  164.4 1.6 convert_element_type.88
  (71 shorter events, 10.6 us)
Async XLA Ops:
  7.2 18.2 %copy-start = (bf16[2304,512]{1,0:T(8,128)(2,1)S(1)}, bf16[2304,512]{1,0:T(8,128)(2,1)}, u32[]{:S(2)}) copy-start(bf16[2304,512]{1,0:T(8,128)(2,1)} %param.10) | copy-start | bytes 7077892
  7.2 27.4 %all-gather.3.cloned.1.call-start = ((), (), s32[]{:S(2)}) async-start(), calls=%async_computation.1 | async-start | bytes 1179648 | tf_op jit(solution)/shard_map/all_gather | solution.py:247
  7.9 156.5 %reduce-scatter.2.cloned.1.call-start = ((), (), s32[]{:S(2)}) async-start(), calls=%async_computation.2 | async-start | bytes 1179648 | tf_op jit(solution)/shard_map/reduce_scatter | solution.py:306
  25.3 9.2 %copy-start.5 = (s32[256]{0:T(256)S(1)}, s32[256]{0:T(256)}, u32[]{:S(2)}) copy-start(s32[256]{0:T(256)} %hb_ref.3) | copy-start | bytes 3076
  36.8 30.7 %copy-start.4 = (bf16[1024,512]{1,0:T(8,128)(2,1)S(1)}, bf16[1024,512]{1,0:T(8,128)(2,1)}, u32[]{:S(2)}) copy-start(bf16[1024,512]{1,0:T(8,128)(2,1)} %get-tuple-element.29) | copy-start | bytes 3145732
  60.1 34.8 %copy-start.1 = (bf16[8,128,512]{2,1,0:T(8,128)(2,1)}, bf16[8,128,512]{2,1,0:T(8,128)(2,1)S(1)}, u32[]{:S(2)}) copy-start(bf16[8,128,512]{2,1,0:T(8,128)(2,1)S(1)} %get-tuple-element.17) | copy-start | bytes 3145732
  60.1 34.7 %collective-permute-start.1 = (bf16[4,128,512]{2,1,0:T(8,128)(2,1)S(1)}, bf16[4,128,512]{2,1,0:T(8,128)(2,1)S(1)}, u32[]{:S(2)}, u32[]{:S(2)}) collective-permute-start(bf16[4,128,512]{2,1,0:T(8,128)(2,1)S(1)} %get-tuple-element.40), channel_id=1, source_target_pairs={{0,16},{8,24},{16,0},{24,8},{1,17},{9,25},{17,1},{25,9},{2,18},{10... | collective-permute-start | bytes 1572872 | tf_op jit(solution)/shard_map/ppermute | solution.py:282
  62.5 32.3 %collective-permute-start = (bf16[4,128,512]{2,1,0:T(8,128)(2,1)S(1)}, bf16[4,128,512]{2,1,0:T(8,128)(2,1)S(1)}, u32[]{:S(2)}, u32[]{:S(2)}) collective-permute-start(bf16[4,128,512]{2,1,0:T(8,128)(2,1)S(1)} %get-tuple-element.41), channel_id=1, source_target_pairs={{0,8},{8,0},{16,24},{24,16},{1,9},{9,1},{17,25},{25,17},{2,10},{10... | collective-permute-start | bytes 1572872 | tf_op jit(solution)/shard_map/ppermute | solution.py:282
  94.5 4.9 %copy-start.3 = (bf16[2048,512]{1,0:T(8,128)(2,1)S(1)}, bf16[2048,512]{1,0:T(8,128)(2,1)}, u32[]{:S(2)}) copy-start(bf16[2048,512]{1,0:T(8,128)(2,1)} %param.9) | copy-start | bytes 6291460
  94.5 4.9 %copy-start.6 = (s32[256]{0:T(256)S(1)}, s32[256]{0:T(256)}, u32[]{:S(2)}) copy-start(s32[256]{0:T(256)} %tb_ref.3) | copy-start | bytes 3076
  94.6 19.3 %collective-permute-start.5 = (bf16[4,128,512]{2,1,0:T(8,128)(2,1)S(1)}, bf16[4,128,512]{2,1,0:T(8,128)(2,1)S(1)}, u32[]{:S(2)}, u32[]{:S(2)}) collective-permute-start(bf16[4,128,512]{2,1,0:T(8,128)(2,1)S(1)} %get-tuple-element.36), channel_id=1, source_target_pairs={{0,16},{8,24},{16,0},{24,8},{1,17},{9,25},{17,1},{25,9},{2,18},{10... | collective-permute-start | bytes 1572872 | tf_op jit(solution)/shard_map/ppermute | solution.py:282
  94.7 19.3 %collective-permute-start.4 = (bf16[4,128,512]{2,1,0:T(8,128)(2,1)S(1)}, bf16[4,128,512]{2,1,0:T(8,128)(2,1)S(1)}, u32[]{:S(2)}, u32[]{:S(2)}) collective-permute-start(bf16[4,128,512]{2,1,0:T(8,128)(2,1)S(1)} %get-tuple-element.37), channel_id=1, source_target_pairs={{0,8},{8,0},{16,24},{24,16},{1,9},{9,1},{17,25},{25,17},{2,10},{10... | collective-permute-start | bytes 1572872 | tf_op jit(solution)/shard_map/ppermute | solution.py:282
  94.8 19.1 %copy-start.9 = (bf16[4,128,512]{2,1,0:T(8,128)(2,1)}, bf16[4,128,512]{2,1,0:T(8,128)(2,1)S(1)}, u32[]{:S(2)}) copy-start(bf16[4,128,512]{2,1,0:T(8,128)(2,1)S(1)} %collective-permute-done.1) | copy-start | bytes 1572868
  94.8 19.1 %copy-start.12 = (bf16[4,128,512]{2,1,0:T(8,128)(2,1)}, bf16[4,128,512]{2,1,0:T(8,128)(2,1)S(1)}, u32[]{:S(2)}) copy-start(bf16[4,128,512]{2,1,0:T(8,128)(2,1)S(1)} %collective-permute-done) | copy-start | bytes 1572868
  95.4 21.7 %collective-permute-start.2 = (bf16[4,128,512]{2,1,0:T(8,128)(2,1)S(1)}, bf16[4,128,512]{2,1,0:T(8,128)(2,1)S(1)}, u32[]{:S(2)}, u32[]{:S(2)}) collective-permute-start(bf16[4,128,512]{2,1,0:T(8,128)(2,1)S(1)} %get-tuple-element.19), channel_id=1, source_target_pairs={{0,16},{8,24},{16,0},{24,8},{1,17},{9,25},{17,1},{25,9},{2,18},{10... | collective-permute-start | bytes 1572872 | tf_op jit(solution)/shard_map/ppermute | solution.py:293
  97.4 21.2 %collective-permute-start.3 = (bf16[4,128,512]{2,1,0:T(8,128)(2,1)S(1)}, bf16[4,128,512]{2,1,0:T(8,128)(2,1)S(1)}, u32[]{:S(2)}, u32[]{:S(2)}) collective-permute-start(bf16[4,128,512]{2,1,0:T(8,128)(2,1)S(1)} %get-tuple-element.20), channel_id=1, source_target_pairs={{0,8},{8,0},{16,24},{24,16},{1,9},{9,1},{17,25},{25,17},{2,10},{10... | collective-permute-start | bytes 1572872 | tf_op jit(solution)/shard_map/ppermute | solution.py:293
  114.0 18.4 %copy-start.10 = (bf16[4,128,512]{2,1,0:T(8,128)(2,1)}, bf16[4,128,512]{2,1,0:T(8,128)(2,1)S(1)}, u32[]{:S(2)}) copy-start(bf16[4,128,512]{2,1,0:T(8,128)(2,1)S(1)} %collective-permute-done.5) | copy-start | bytes 1572868
  114.0 18.4 %copy-start.13 = (bf16[4,128,512]{2,1,0:T(8,128)(2,1)}, bf16[4,128,512]{2,1,0:T(8,128)(2,1)S(1)}, u32[]{:S(2)}) copy-start(bf16[4,128,512]{2,1,0:T(8,128)(2,1)S(1)} %collective-permute-done.4) | copy-start | bytes 1572868
  117.1 15.3 %copy-start.15 = (bf16[4,128,512]{2,1,0:T(8,128)(2,1)}, bf16[4,128,512]{2,1,0:T(8,128)(2,1)S(1)}, u32[]{:S(2)}) copy-start(bf16[4,128,512]{2,1,0:T(8,128)(2,1)S(1)} %collective-permute-done.2) | copy-start | bytes 1572868
  118.6 13.8 %copy-start.16 = (bf16[4,128,512]{2,1,0:T(8,128)(2,1)}, bf16[4,128,512]{2,1,0:T(8,128)(2,1)S(1)}, u32[]{:S(2)}) copy-start(bf16[4,128,512]{2,1,0:T(8,128)(2,1)S(1)} %collective-permute-done.3) | copy-start | bytes 1572868
  133.5 13.1 %copy-start.11 = (bf16[4,128,512]{2,1,0:T(8,128)(2,1)S(1)}, bf16[4,128,512]{2,1,0:T(8,128)(2,1)}, u32[]{:S(2)}) copy-start(bf16[4,128,512]{2,1,0:T(8,128)(2,1)} %copy-done.10) | copy-start | bytes 1572868
  133.5 13.1 %copy-start.14 = (bf16[4,128,512]{2,1,0:T(8,128)(2,1)S(1)}, bf16[4,128,512]{2,1,0:T(8,128)(2,1)}, u32[]{:S(2)}) copy-start(bf16[4,128,512]{2,1,0:T(8,128)(2,1)} %copy-done.13) | copy-start | bytes 1572868
  133.5 12.7 %collective-permute-start.6 = (bf16[4,128,512]{2,1,0:T(8,128)(2,1)}, bf16[4,128,512]{2,1,0:T(8,128)(2,1)S(1)}, u32[]{:S(2)}, u32[]{:S(2)}) collective-permute-start(bf16[4,128,512]{2,1,0:T(8,128)(2,1)} %get-tuple-element.26), channel_id=1, source_target_pairs={{0,16},{8,24},{16,0},{24,8},{1,17},{9,25},{17,1},{25,9},{2,18},{10... | collective-permute-start | bytes 1572872 | tf_op jit(solution)/shard_map/ppermute | solution.py:293
  136.2 10.4 %collective-permute-start.7 = (bf16[4,128,512]{2,1,0:T(8,128)(2,1)}, bf16[4,128,512]{2,1,0:T(8,128)(2,1)S(1)}, u32[]{:S(2)}, u32[]{:S(2)}) collective-permute-start(bf16[4,128,512]{2,1,0:T(8,128)(2,1)} %get-tuple-element.27), channel_id=1, source_target_pairs={{0,8},{8,0},{16,24},{24,16},{1,9},{9,1},{17,25},{25,17},{2,10},{10... | collective-permute-start | bytes 1572872 | tf_op jit(solution)/shard_map/ppermute | solution.py:293
  (3 other events, 5.2 us)
Sparse Core Ops, SparseCore 0:
  9.6 24.8 all-gather.2
  133.6 30.7 reduce-scatter.1

commit v3 on v2

--- a/solution.py
+++ b/solution.py
@@ -297,12 +297,15 @@
     slopes, *onwards[:early] = lax.optimization_barrier((slopes, *onwards[:early]))
     lasts = [onward_step(i, v) for i, v in enumerate(onwards[:early])]
     low = head_pass(0, part, 2, by_head, head_starts, tail_block, tails3, rel, slopes)
-    slopes, low, lasts, onwards = lax.optimization_barrier((slopes, low, lasts, onwards))
+    slopes, low, onwards = lax.optimization_barrier((slopes, low, onwards))
     lasts = lasts + [onward_step(i, onwards[i]) for i in range(early, len(onwards))]
+    more = (members - part) * 3 // 4
+    mid = head_pass(part, more, 3, by_head, head_starts, tail_block, tails3, rel, slopes)
+    slopes, mid, lasts = lax.optimization_barrier((slopes, mid, lasts))
     high = head_pass(
-        part, members - part, 2, by_head, head_starts, tail_block, tails3, rel, slopes
+        part + more, members - part - more, 8, by_head, head_starts, tail_block, tails3, rel, slopes
     )
-    head_local = jnp.concatenate([low, high], axis=0)
+    head_local = jnp.concatenate([low, mid, high], axis=0)
     head_grad = lax.psum_scatter(
         head_local.reshape(members * rows, width), "blk", scatter_dimension=0, tiled=True
     ).astype(jnp.float32)

time: 173 us -> 174 us (level)
  waiting for transfers between devices: 31.5 us -> 34.6 us
  starting transfers between devices: 14.6 us -> 11.8 us
    reduce_scatter x1, waiting for transfers between devices: 14.6 us -> 24.7 us  [on_device(): lax.psum_scatter(head_local.reshape(members * rows, width), 'blk', scatte...]
    ppermute x4, waiting for transfers between devices: 10.6 us -> 4.03 us  [onward_step(): return lax.ppermute(value, 'grp', [(g, g ^ far) for g in range(groups)])]
    pallas_call x2, Pallas kernels: 50.2 us -> 47.3 us  [tail_chunk(): pl.pallas_call(functools.partial(tail_kernel, first), out_shape=[jax.Shap...]
    ppermute x4, starting transfers between devices: 6.96 us -> 4.93 us  [onward_step(): return lax.ppermute(value, 'grp', [(g, g ^ far) for g in range(groups)])]
    pallas_call x2 -> x3, Pallas kernels: 28.3 us -> 29.9 us  [head_pass(): pl.pallas_call(functools.partial(head_kernel, first), out_shape=jax.Shape...]
    unnamed x37 -> x49, local copies, waits for them, and re-layouts: 4.33 us -> 5.58 us
  transfers between devices with their start and end apart: 10 -> 10, of which waited for: 6 -> 4; matrix products, arithmetic and copies ran while one was open for 11% -> 11% of each run, Pallas kernels for 24% -> 28%
where the time goes in v3:
time: 174 us; the launch traced here: 173 us
  Pallas kernels  77.2 us (44%)
  waiting for transfers between devices  34.6 us (20%)
  other arithmetic  15.3 us (9%)
  between operations  15.1 us (9%)
  starting transfers between devices  11.8 us (7%)
  blocking collectives  8.82 us (5%)
  local copies, waits for them, and re-layouts  7.32 us (4%)
  matrix products  2.5 us (1%)
    pallas_call x2, Pallas kernels, tail_chunk(): pl.pallas_call(functools.partial(tail_kernel, first), out_shape=[jax.Shap...  47.3 us
    pallas_call x3, Pallas kernels, head_pass(): pl.pallas_call(functools.partial(head_kernel, first), out_shape=jax.Shape...  29.9 us
    reduce_scatter x1, waiting for transfers between devices, on_device(): lax.psum_scatter(head_local.reshape(members * rows, width), 'blk', scatte...  24.7 us
    unnamed x1, blocking collectives  8.82 us
    ppermute x4, starting transfers between devices, on_device(): theirs = lax.ppermute(mine, 'grp', [(g, g ^ near) for g in range(groups)])  6.81 us
    unnamed x49, local copies, waits for them, and re-layouts  5.58 us
    all_gather x1, waiting for transfers between devices, on_device(): lax.all_gather(heads, 'blk', axis=0, tiled=True)  5.23 us
    ppermute x4, starting transfers between devices, onward_step(): return lax.ppermute(value, 'grp', [(g, g ^ far) for g in range(groups)])  4.93 us
  transfers between devices with their start and end apart: 10, of which 4 were waited for; matrix products, arithmetic and copies ran while one was open for 11% of the time, Pallas kernels for 28%

profile of v3, /device:TPU:0, one launch (start us, length us, event | category | flops | bytes accessed | tf_op | source)
XLA Modules:
  0.0 172.8 jit_solution(1570874831028135704)
XLA Ops:
  13.2 1.2 dynamic-slice
  15.9 8.8 %all-reduce = s32[64]{0:T(128)S(1)} all-reduce(s32[64]{0:T(128)S(1)} %bitcast_dynamic-update-slice_fusion), channel_id=2, replica_groups=mesh['grp'=4,'blk'=8] {'grp'}, use_global_device_ids=true, to_apply=%add | all-reduce | flops 64 | bytes 512
  25.3 2.5 %fusion.rel_ref = f32[256,512]{1,0:T(8,128)} fusion(bf16[2304,512]{1,0:T(8,128)(2,1)S(1)} %copy-done, s32[256]{0:T(256)} %param.13), kind=kOutput, calls=%fused_computation.2 | convolution fusion | flops 604569600 | bytes 2884608 | tf_op jit(solution)/shard_map/dot_general | solution.py:252
  27.8 1.5 fusion.20
  29.3 5.2 %all-gather.3.cloned.1.call-done = bf16[1024,512]{1,0:T(8,128)(2,1)} async-done(((bf16[128,512]{1,0:T(8,128)(2,1)}), bf16[1024,512]{1,0:T(8,128)(2,1)}) %all-gather.3.cloned.1.call-update) | async-done | bytes 1048592 | tf_op jit(solution)/shard_map/all_gather | solution.py:247
  34.5 1.2 copy-done.5
  35.8 1.2 copy-done.8
  38.0 23.7 %tail_chunk.2 = (bf16[8,128,512]{2,1,0:T(8,128)(2,1)S(1)}, bf16[257,128,128]{2,1,0:T(8,128)(2,1)S(1)}) custom-call(s32[384]{0:T(512)S(1)} %broadcast_add_fusion.1.list_ref, s32[17]{0:T(128)S(1)} %select_reduce_fusion.4.gs_ref, s32[256]{0:T(256)S(1)} %copy-done.6, bf16[8,128,512]{2,1,0:T(8,128)(2,1)S(1)} %bitcast.47, bf16[8,128,512]{2,1,0:T(8,128)(2,1)S(1)} %bitcast.46, ...), custom_call_target="tpu_custom_call" | custom-call | flops 27917287424 | bytes 12582912 | tf_op jit(solution)/shard_map/tail_chunk/pallas_call | solution.py:192
  61.8 2.4 %collective-permute-start.1 = (bf16[4,128,512]{2,1,0:T(8,128)(2,1)S(1)}, bf16[4,128,512]{2,1,0:T(8,128)(2,1)S(1)}, u32[]{:S(2)}, u32[]{:S(2)}) collective-permute-start(bf16[4,128,512]{2,1,0:T(8,128)(2,1)S(1)} %get-tuple-element.48), channel_id=1, source_target_pairs={{0,16},{8,24},{16,0},{24,8},{1,17},{9,25},{17,1},{25,9},{2,18},{10... | collective-permute-start | bytes 1572872 | tf_op jit(solution)/shard_map/ppermute | solution.py:282
  64.2 1.5 collective-permute-start
  65.7 23.7 %tail_chunk.3 = (bf16[8,128,512]{2,1,0:T(8,128)(2,1)S(1)}, bf16[257,128,128]{2,1,0:T(8,128)(2,1)S(1)}) custom-call(s32[384]{0:T(512)S(1)} %broadcast_add_fusion.1.list_ref, s32[17]{0:T(128)S(1)} %select_reduce_fusion.4.gs_ref, s32[256]{0:T(256)S(1)} %copy-done.6, bf16[8,128,512]{2,1,0:T(8,128)(2,1)S(1)} %bitcast.48, ...), custom_call_target="tpu_custom_call", output_to_operand_aliasing={{1}: (7, {})} | custom-call | flops 27917287424 | bytes 12582912 | tf_op jit(solution)/shard_map/tail_chunk/pallas_call | solution.py:192
  89.6 2.9 %collective-permute-start.2 = (bf16[4,128,512]{2,1,0:T(8,128)(2,1)S(1)}, bf16[4,128,512]{2,1,0:T(8,128)(2,1)S(1)}, u32[]{:S(2)}, u32[]{:S(2)}) collective-permute-start(bf16[4,128,512]{2,1,0:T(8,128)(2,1)S(1)} %get-tuple-element.45), channel_id=1, source_target_pairs={{0,8},{8,0},{16,24},{24,16},{1,9},{9,1},{17,25},{25,17},{2,10},{10... | collective-permute-start | bytes 1572872 | tf_op jit(solution)/shard_map/ppermute | solution.py:282
  93.0 2.0 %collective-permute-start.4 = (bf16[4,128,512]{2,1,0:T(8,128)(2,1)S(1)}, bf16[4,128,512]{2,1,0:T(8,128)(2,1)S(1)}, u32[]{:S(2)}, u32[]{:S(2)}) collective-permute-start(bf16[4,128,512]{2,1,0:T(8,128)(2,1)S(1)} %get-tuple-element.23), channel_id=1, source_target_pairs={{0,16},{8,24},{16,0},{24,8},{1,17},{9,25},{17,1},{25,9},{2,18},{10... | collective-permute-start | bytes 1572872 | tf_op jit(solution)/shard_map/ppermute | solution.py:293
  95.0 14.5 %head_pass.3 = bf16[4,128,512]{2,1,0:T(8,128)(2,1)S(1)} custom-call(s32[320]{0:T(512)S(1)} %broadcast_add_fusion.list_ref, s32[9]{0:T(128)S(1)} %select_reduce_fusion.5.gs_ref, s32[256]{0:T(256)S(1)} %copy-done.7, bf16[16,128,512]{2,1,0:T(8,128)(2,1)S(1)} %bitcast.42, f32[256,512]{1,0:T(8,128)S(1)} %copy-done.10, ...), custom_call_target="tpu_custom_call" | custom-call | flops 17179869184 | bytes 4194304 | tf_op jit(solution)/shard_map/head_pass/pallas_call | solution.py:221
  111.1 1.9 %collective-permute-start.7 = (bf16[4,128,512]{2,1,0:T(8,128)(2,1)S(1)}, bf16[4,128,512]{2,1,0:T(8,128)(2,1)S(1)}, u32[]{:S(2)}, u32[]{:S(2)}) collective-permute-start(bf16[4,128,512]{2,1,0:T(8,128)(2,1)S(1)} %get-tuple-element.29), channel_id=1, source_target_pairs={{0,8},{8,0},{16,24},{24,16},{1,9},{9,1},{17,25},{25,17},{2,10},{10... | collective-permute-start | bytes 1572872 | tf_op jit(solution)/shard_map/ppermute | solution.py:293
  113.1 10.0 %head_pass.4 = bf16[3,128,512]{2,1,0:T(8,128)(2,1)S(1)} custom-call(s32[320]{0:T(512)S(1)} %broadcast_add_fusion.list_ref, s32[9]{0:T(128)S(1)} %select_reduce_fusion.5.gs_ref, s32[256]{0:T(256)S(1)} %copy-done.7, bf16[16,128,512]{2,1,0:T(8,128)(2,1)S(1)} %bitcast.43, f32[256,512]{1,0:T(8,128)S(1)} %copy-done.10, ...), custom_call_target="tpu_custom_call" | custom-call | flops 11408506880 | bytes 2785280 | tf_op jit(solution)/shard_map/head_pass/pallas_call | solution.py:221
  123.1 2.6 %collective-permute-done.6 = bf16[4,128,512]{2,1,0:T(8,128)(2,1)S(1)} collective-permute-done((bf16[4,128,512]{2,1,0:T(8,128)(2,1)S(1)}, bf16[4,128,512]{2,1,0:T(8,128)(2,1)S(1)}, u32[]{:S(2)}, u32[]{:S(2)}) %collective-permute-start.6) | collective-permute-done | bytes 524320 | tf_op jit(solution)/shard_map/ppermute | solution.py:293
  125.8 1.4 collective-permute-done.7
  127.2 5.4 %head_pass.5 = bf16[1,128,512]{2,1,0:T(8,128)(2,1)S(1)} custom-call(s32[320]{0:T(512)S(1)} %broadcast_add_fusion.list_ref, s32[9]{0:T(128)S(1)} %select_reduce_fusion.5.gs_ref, s32[256]{0:T(256)S(1)} %copy-done.7, bf16[16,128,512]{2,1,0:T(8,128)(2,1)S(1)} %bitcast.44, f32[256,512]{1,0:T(8,128)S(1)} %copy-done.10, ...), custom_call_target="tpu_custom_call" | custom-call | flops 4294967296 | bytes 1048576 | tf_op jit(solution)/shard_map/head_pass/pallas_call | solution.py:221
  132.6 1.1 pad_maximum_fusion.1
  133.8 2.6 %fusion.13 = (f32[4,128,512]{2,1,0:T(8,128)S(1)}, f32[4,128,512]{2,1,0:T(8,128)S(1)}) fusion(bf16[4,128,512]{2,1,0:T(8,128)(2,1)} %copy-done.16, bf16[4,128,512]{2,1,0:T(8,128)(2,1)} %copy-done.21, pred[4]{0:T(512)(128)(4,1)S(1)} %get-tuple-element.73, pred[4]{0:T(512)(128)(4,1)S(1)} %get-tuple-element.55, bf16[8,128,512]{2,1,0:T(8,128)(2,1)} %copy-done.1, ...), kind=kLoop, calls=%fused_computation.31 | loop fusion | flops 3670016 | bytes 5242896 | tf_op jit(solution)/shard_map/add | solution.py:316
  137.0 2.6 %pad_maximum_fusion = f32[16,128,512]{2,1,0:T(8,128)} fusion(f32[4,128,512]{2,1,0:T(8,128)S(1)} %get-tuple-element.41, f32[4,128,512]{2,1,0:T(8,128)S(1)} %get-tuple-element.40, f32[4,128,512]{2,1,0:T(8,128)S(1)} %get-tuple-element.39, f32[4,128,512]{2,1,0:T(8,128)S(1)} %get-tuple-element.38), kind=kLoop, calls=%fused_computation | loop fusion | flops 3145728 | bytes 8388608 | tf_op jit(solution)/shard_map/concatenate | solution.py:320
  139.6 24.7 %reduce-scatter.2.cloned.1.call-done = bf16[128,512]{1,0:T(8,128)(2,1)} async-done(((bf16[1024,512]{1,0:T(8,128)(2,1)}), bf16[128,512]{1,0:T(8,128)(2,1)}) %reduce-scatter.2.cloned.1.call-update) | async-done | bytes 131088 | tf_op jit(solution)/shard_map/reduce_scatter | solution.py:309
  164.3 1.6 convert_element_type.88
  (84 shorter events, 11.4 us)
Async XLA Ops:
  7.2 18.2 %copy-start = (bf16[2304,512]{1,0:T(8,128)(2,1)S(1)}, bf16[2304,512]{1,0:T(8,128)(2,1)}, u32[]{:S(2)}) copy-start(bf16[2304,512]{1,0:T(8,128)(2,1)} %param.10) | copy-start | bytes 7077892
  7.2 27.4 %all-gather.3.cloned.1.call-start = ((), (), s32[]{:S(2)}) async-start(), calls=%async_computation.1 | async-start | bytes 1179648 | tf_op jit(solution)/shard_map/all_gather | solution.py:247
  7.9 156.4 %reduce-scatter.2.cloned.1.call-start = ((), (), s32[]{:S(2)}) async-start(), calls=%async_computation.2 | async-start | bytes 1179648 | tf_op jit(solution)/shard_map/reduce_scatter | solution.py:309
  25.3 9.2 %copy-start.6 = (s32[256]{0:T(256)S(1)}, s32[256]{0:T(256)}, u32[]{:S(2)}) copy-start(s32[256]{0:T(256)} %hb_ref.3) | copy-start | bytes 3076
  38.0 27.7 %copy-start.4 = (bf16[1024,512]{1,0:T(8,128)(2,1)S(1)}, bf16[1024,512]{1,0:T(8,128)(2,1)}, u32[]{:S(2)}) copy-start(bf16[1024,512]{1,0:T(8,128)(2,1)} %get-tuple-element.37) | copy-start | bytes 3145732
  61.8 30.6 %collective-permute-start.1 = (bf16[4,128,512]{2,1,0:T(8,128)(2,1)S(1)}, bf16[4,128,512]{2,1,0:T(8,128)(2,1)S(1)}, u32[]{:S(2)}, u32[]{:S(2)}) collective-permute-start(bf16[4,128,512]{2,1,0:T(8,128)(2,1)S(1)} %get-tuple-element.48), channel_id=1, source_target_pairs={{0,16},{8,24},{16,0},{24,8},{1,17},{9,25},{17,1},{25,9},{2,18},{10... | collective-permute-start | bytes 1572872 | tf_op jit(solution)/shard_map/ppermute | solution.py:282
  64.2 28.2 %collective-permute-start = (bf16[4,128,512]{2,1,0:T(8,128)(2,1)S(1)}, bf16[4,128,512]{2,1,0:T(8,128)(2,1)S(1)}, u32[]{:S(2)}, u32[]{:S(2)}) collective-permute-start(bf16[4,128,512]{2,1,0:T(8,128)(2,1)S(1)} %get-tuple-element.49), channel_id=1, source_target_pairs={{0,8},{8,0},{16,24},{24,16},{1,9},{9,1},{17,25},{25,17},{2,10},{10... | collective-permute-start | bytes 1572872 | tf_op jit(solution)/shard_map/ppermute | solution.py:282
  89.4 20.2 %copy-start.1 = (bf16[8,128,512]{2,1,0:T(8,128)(2,1)}, bf16[8,128,512]{2,1,0:T(8,128)(2,1)S(1)}, u32[]{:S(2)}) copy-start(bf16[8,128,512]{2,1,0:T(8,128)(2,1)S(1)} %get-tuple-element.25) | copy-start | bytes 3145732
  89.4 5.6 %copy-start.3 = (bf16[2048,512]{1,0:T(8,128)(2,1)S(1)}, bf16[2048,512]{1,0:T(8,128)(2,1)}, u32[]{:S(2)}) copy-start(bf16[2048,512]{1,0:T(8,128)(2,1)} %param.9) | copy-start | bytes 6291460
  89.4 5.6 %copy-start.7 = (s32[256]{0:T(256)S(1)}, s32[256]{0:T(256)}, u32[]{:S(2)}) copy-start(s32[256]{0:T(256)} %tb_ref.5) | copy-start | bytes 3076
  89.4 5.6 %copy-start.10 = (f32[256,512]{1,0:T(8,128)S(1)}, f32[256,512]{1,0:T(8,128)}, u32[]{:S(2)}) copy-start(f32[256,512]{1,0:T(8,128)} %fusion.rel_ref) | copy-start | bytes 1572868
  89.5 20.1 %collective-permute-start.3 = (bf16[4,128,512]{2,1,0:T(8,128)(2,1)S(1)}, bf16[4,128,512]{2,1,0:T(8,128)(2,1)S(1)}, u32[]{:S(2)}, u32[]{:S(2)}) collective-permute-start(bf16[4,128,512]{2,1,0:T(8,128)(2,1)S(1)} %get-tuple-element.44), channel_id=1, source_target_pairs={{0,16},{8,24},{16,0},{24,8},{1,17},{9,25},{17,1},{25,9},{2,18},{10... | collective-permute-start | bytes 1572872 | tf_op jit(solution)/shard_map/ppermute | solution.py:282
  89.6 20.0 %collective-permute-start.2 = (bf16[4,128,512]{2,1,0:T(8,128)(2,1)S(1)}, bf16[4,128,512]{2,1,0:T(8,128)(2,1)S(1)}, u32[]{:S(2)}, u32[]{:S(2)}) collective-permute-start(bf16[4,128,512]{2,1,0:T(8,128)(2,1)S(1)} %get-tuple-element.45), channel_id=1, source_target_pairs={{0,8},{8,0},{16,24},{24,16},{1,9},{9,1},{17,25},{25,17},{2,10},{10... | collective-permute-start | bytes 1572872 | tf_op jit(solution)/shard_map/ppermute | solution.py:282
  92.4 17.1 %copy-start.13 = (bf16[4,128,512]{2,1,0:T(8,128)(2,1)}, bf16[4,128,512]{2,1,0:T(8,128)(2,1)S(1)}, u32[]{:S(2)}) copy-start(bf16[4,128,512]{2,1,0:T(8,128)(2,1)S(1)} %collective-permute-done) | copy-start | bytes 1572868
  93.0 30.1 %collective-permute-start.4 = (bf16[4,128,512]{2,1,0:T(8,128)(2,1)S(1)}, bf16[4,128,512]{2,1,0:T(8,128)(2,1)S(1)}, u32[]{:S(2)}, u32[]{:S(2)}) collective-permute-start(bf16[4,128,512]{2,1,0:T(8,128)(2,1)S(1)} %get-tuple-element.23), channel_id=1, source_target_pairs={{0,16},{8,24},{16,0},{24,8},{1,17},{9,25},{17,1},{25,9},{2,18},{10... | collective-permute-start | bytes 1572872 | tf_op jit(solution)/shard_map/ppermute | solution.py:293
  95.0 28.1 %collective-permute-start.5 = (bf16[4,128,512]{2,1,0:T(8,128)(2,1)S(1)}, bf16[4,128,512]{2,1,0:T(8,128)(2,1)S(1)}, u32[]{:S(2)}, u32[]{:S(2)}) collective-permute-start(bf16[4,128,512]{2,1,0:T(8,128)(2,1)S(1)} %get-tuple-element.24), channel_id=1, source_target_pairs={{0,8},{8,0},{16,24},{24,16},{1,9},{9,1},{17,25},{25,17},{2,10},{10... | collective-permute-start | bytes 1572872 | tf_op jit(solution)/shard_map/ppermute | solution.py:293
  109.6 13.5 %copy-start.15 = (bf16[4,128,512]{2,1,0:T(8,128)(2,1)}, bf16[4,128,512]{2,1,0:T(8,128)(2,1)S(1)}, u32[]{:S(2)}) copy-start(bf16[4,128,512]{2,1,0:T(8,128)(2,1)S(1)} %collective-permute-done.3) | copy-start | bytes 1572868
  109.6 13.5 %copy-start.16 = (bf16[4,128,512]{2,1,0:T(8,128)(2,1)}, bf16[4,128,512]{2,1,0:T(8,128)(2,1)S(1)}, u32[]{:S(2)}) copy-start(bf16[4,128,512]{2,1,0:T(8,128)(2,1)S(1)} %collective-permute-done.2) | copy-start | bytes 1572868
  110.2 15.6 %collective-permute-start.6 = (bf16[4,128,512]{2,1,0:T(8,128)(2,1)S(1)}, bf16[4,128,512]{2,1,0:T(8,128)(2,1)S(1)}, u32[]{:S(2)}, u32[]{:S(2)}) collective-permute-start(bf16[4,128,512]{2,1,0:T(8,128)(2,1)S(1)} %get-tuple-element.28), channel_id=1, source_target_pairs={{0,16},{8,24},{16,0},{24,8},{1,17},{9,25},{17,1},{25,9},{2,18},{10... | collective-permute-start | bytes 1572872 | tf_op jit(solution)/shard_map/ppermute | solution.py:293
  111.1 16.0 %collective-permute-start.7 = (bf16[4,128,512]{2,1,0:T(8,128)(2,1)S(1)}, bf16[4,128,512]{2,1,0:T(8,128)(2,1)S(1)}, u32[]{:S(2)}, u32[]{:S(2)}) collective-permute-start(bf16[4,128,512]{2,1,0:T(8,128)(2,1)S(1)} %get-tuple-element.29), channel_id=1, source_target_pairs={{0,8},{8,0},{16,24},{24,16},{1,9},{9,1},{17,25},{25,17},{2,10},{10... | collective-permute-start | bytes 1572872 | tf_op jit(solution)/shard_map/ppermute | solution.py:293
  123.1 9.5 %copy-start.17 = (bf16[4,128,512]{2,1,0:T(8,128)(2,1)}, bf16[4,128,512]{2,1,0:T(8,128)(2,1)S(1)}, u32[]{:S(2)}) copy-start(bf16[4,128,512]{2,1,0:T(8,128)(2,1)S(1)} %collective-permute-done.4) | copy-start | bytes 1572868
  123.1 9.5 %copy-start.19 = (bf16[4,128,512]{2,1,0:T(8,128)(2,1)}, bf16[4,128,512]{2,1,0:T(8,128)(2,1)S(1)}, u32[]{:S(2)}) copy-start(bf16[4,128,512]{2,1,0:T(8,128)(2,1)S(1)} %collective-permute-done.5) | copy-start | bytes 1572868
  125.8 6.8 %copy-start.21 = (bf16[4,128,512]{2,1,0:T(8,128)(2,1)}, bf16[4,128,512]{2,1,0:T(8,128)(2,1)S(1)}, u32[]{:S(2)}) copy-start(bf16[4,128,512]{2,1,0:T(8,128)(2,1)S(1)} %collective-permute-done.6) | copy-start | bytes 1572868
  127.2 5.5 %copy-start.22 = (bf16[4,128,512]{2,1,0:T(8,128)(2,1)}, bf16[4,128,512]{2,1,0:T(8,128)(2,1)S(1)}, u32[]{:S(2)}) copy-start(bf16[4,128,512]{2,1,0:T(8,128)(2,1)S(1)} %collective-permute-done.7) | copy-start | bytes 1572868
  (9 other events, 19.4 us)
Sparse Core Ops, SparseCore 0:
  9.6 24.8 all-gather.2
  133.9 30.3 reduce-scatter.1
